TPU v7x, 32 devices: a whole 2x2x4 slice. The times are simulated.
32 devices in a mesh: dp: 2 (over y), label: 8 (over z, x), tensor: 2 (over core).
Axes of the slice: x: 2, y: 2, z: 4, core: 2. Of those that a mesh axis runs over, the one named last changes fastest.
Arguments:
- hidden: bfloat16 [2048, 3584], P('dp', 'label'), may hold values from -6 to 6
- enc_weight: bfloat16 [3584, 3584], P('label', 'tensor'), may hold values from -0.09375 to 0.09375
- enc_gain: float32 [3584], P('tensor'), may hold values from 0.25 to 1.75
- head_weight: bfloat16 [16, 256, 3584], P('label', None, 'tensor'), may hold values from -0.09375 to 0.09375
- propensity: float32 [16, 256], P('label'), may hold values from 0.25 to 1
- blocks: int32 [2048, 8], P(('dp', 'label')), may hold values from 0 to 15, all different within a row; in each aligned block of 128 rows (0 to 127, 128 to 255, ...) at most 128 rows name the same one
- offsets: int32 [2048, 2], P(('dp', 'label')), may hold values from 0 to 255
Outputs:
- enc_grad: float32 [3584, 3584], P('label', 'tensor')
- head_grad: float32 [16, 256, 3584], P('label', 'dp', 'tensor')
Inputs may be any that keep to these rules, and one draw needn't show every extreme that they name: Each row names 8 different blocks. Among the rows of one device no block is named more than 128 times, and in every draw some block is named exactly 128 times by the rows of some device.
All inputs are finite; a program needn't handle non-finite values.
Results may differ from a plain program's by a relative error of at most 0.014.
Values may be sent and summed in bfloat16 or wider, within the bound.
A program may use at most 128 MiB of HBM per device.

v0:
```python
import jax
import jax.numpy as jnp
from jax import lax
from jax.sharding import PartitionSpec as P

EPSILON = 1e-06


def round_keep(values_in):
    rounded = lax.optimization_barrier(values_in.astype(jnp.bfloat16))
    return rounded.astype(jnp.float32)


def shards(hidden, enc_weight, enc_gain, head_weight, propensity, blocks, offsets):
    labels_n = lax.axis_size("label")
    width_half = enc_weight.shape[1]
    shard_rows = enc_weight.shape[0]
    rows_here = blocks.shape[0]
    slots = blocks.shape[1]
    pos_count = offsets.shape[1]
    blocks_dev = head_weight.shape[0]
    block_size = head_weight.shape[1]
    total_blocks = blocks_dev * labels_n
    capacity = max(2, min(rows_here, 2 * rows_here * slots // total_blocks))
    full_width = width_half * lax.axis_size("tensor")
    row_features = lax.all_to_all(hidden, "label", split_axis=0, concat_axis=1, tiled=True)
    shard_piece = lax.all_gather(enc_weight, "label", axis=0, tiled=True)
    piece_count = shard_piece.shape[0] // shard_rows
    products = jnp.einsum(
        "imr,mrd->mid",
        row_features.reshape(rows_here, piece_count, shard_rows),
        shard_piece.reshape(piece_count, shard_rows, width_half),
        preferred_element_type=jnp.float32,
    )
    pooled = jnp.sum(round_keep(products), axis=0)
    squares = lax.psum(jnp.sum(pooled * pooled, axis=1), "tensor")
    inverse = lax.rsqrt(squares / full_width + EPSILON)
    embedded = (pooled * inverse[:, None] * enc_gain[None, :]).astype(jnp.bfloat16)
    requests = blocks.reshape(-1)
    request_count = rows_here * slots
    match_table = (requests[:, None] == jnp.arange(total_blocks, dtype=jnp.int32)[None, :]).astype(
        jnp.int32
    )
    earlier = jnp.cumsum(match_table, axis=0) - match_table
    position = jnp.sum(earlier * match_table, axis=1)
    dest_slot = requests * capacity + position
    slot_source = (
        jnp.zeros((total_blocks * capacity,), jnp.int32)
        .at[dest_slot]
        .set(jnp.arange(request_count, dtype=jnp.int32) + 1)
    )
    filled = slot_source > 0
    source = jnp.maximum(slot_source - 1, 0)
    src_row = source // slots
    src_slot = source % slots
    send_rows = jnp.where(filled[:, None], embedded[src_row], jnp.zeros((), jnp.bfloat16))
    offset_pick = offsets[src_row, jnp.minimum(src_slot, pos_count - 1)]
    target = jnp.where(src_slot < pos_count, offset_pick, -1)
    target = jnp.where(filled, target, -2)
    per_owner = blocks_dev * capacity
    recv_rows, recv_target = (
        lax.all_to_all(
            send_rows.reshape(labels_n, per_owner, width_half),
            "label",
            split_axis=0,
            concat_axis=0,
            tiled=True,
        ),
        lax.all_to_all(
            target.reshape(labels_n, per_owner), "label", split_axis=0, concat_axis=0, tiled=True
        ),
    )
    recv_four = recv_rows.reshape(labels_n, blocks_dev, capacity, width_half)
    target_four = recv_target.reshape(labels_n, blocks_dev, capacity)
    partial_scores = jnp.einsum(
        "snmd,njd->snmj", recv_four, head_weight, preferred_element_type=jnp.float32
    )
    scores = lax.psum(partial_scores.astype(jnp.bfloat16), "tensor").astype(jnp.float32)
    label_ids = jnp.arange(block_size, dtype=jnp.int32)
    is_positive = target_four[..., None] == label_ids
    is_valid = (target_four > -2)[..., None]
    weight_pos = (1.0 / propensity)[None, :, None, :]
    above = jnp.maximum(1.0 - scores, 0.0)
    below = jnp.maximum(1.0 + scores, 0.0)
    slopes = jnp.where(
        is_positive, -2.0 * weight_pos * above + 2.0 * (1.0 - weight_pos) * below, 2.0 * below
    )
    slopes = jnp.where(is_valid, slopes / rows_here, 0.0).astype(jnp.bfloat16)
    back_terms = jnp.einsum(
        "snmj,njd->snmd", slopes, head_weight, preferred_element_type=jnp.float32
    ).astype(jnp.bfloat16)
    returned = lax.all_to_all(
        back_terms.reshape(labels_n, per_owner, width_half),
        "label",
        split_axis=0,
        concat_axis=0,
        tiled=True,
    )
    slot_grads = returned.reshape(total_blocks * capacity, width_half)[dest_slot]
    embed_grad = jnp.sum(
        slot_grads.reshape(rows_here, slots, width_half).astype(jnp.float32), axis=1
    )
    head_partial = jnp.einsum(
        "snmj,snmd->njd", slopes, recv_four, preferred_element_type=jnp.float32
    )
    head_grad = lax.psum_scatter(
        head_partial.astype(jnp.bfloat16), "dp", scatter_dimension=1, tiled=True
    ).astype(jnp.float32)
    scaled = embed_grad * enc_gain[None, :]
    row_dot = lax.psum(jnp.sum(scaled * pooled, axis=1), "tensor")
    pooled_grad = (
        inverse[:, None] * (scaled - pooled * (inverse * inverse * row_dot / full_width)[:, None])
    ).astype(jnp.bfloat16)
    weight_part = lax.dot_general(
        hidden,
        lax.all_gather(pooled_grad, "label", axis=0, tiled=True),
        (((0,), (0,)), ((), ())),
        preferred_element_type=jnp.float32,
    )
    enc_grad = lax.psum(weight_part.astype(jnp.bfloat16), "dp").astype(jnp.float32)
    return (enc_grad, head_grad)


def solution(mesh):
    in_specs = (
        P("dp", "label"),
        P("label", "tensor"),
        P("tensor"),
        P("label", None, "tensor"),
        P("label", None),
        P(("dp", "label"), None),
        P(("dp", "label"), None),
    )
    out_specs = (P("label", "tensor"), P("label", "dp", "tensor"))
    return jax.shard_map(shards, mesh=mesh, in_specs=in_specs, out_specs=out_specs, check_vma=False)
```

profile of v0, /device:TPU:0, one launch (start us, length us, event | category | flops | bytes accessed | tf_op | source)
XLA Modules:
  0.0 774.5 jit_solution(10302828192113432690)
XLA Ops:
  9.6 7.3 all-to-all-start
  17.4 4.5 reduce-window.6
  22.4 4.3 scatter_custom_fusion
  26.8 16.9 %gather_fusion = s32[2048]{0:T(1024)S(1)} fusion(s32[128,2]{0,1:T(2,128)S(1)} %copy-done.2, s32[2048]{0:T(1024)S(1)} %fusion.36), kind=kCustom, calls=%fused_computation | custom fusion | bytes 32768 | tf_op jit(solution)/shard_map/gather | solution.py:57
  44.3 15.4 %all-to-all-done = bf16[8,128,448]{1,2,0:T(8,128)(2,1)S(1)} async-done(((bf16[8,128,448]{1,2,0:T(8,128)(2,1)}), bf16[8,128,448]{1,2,0:T(8,128)(2,1)S(1)}, u32[]{:S(2)}, u32[]{:S(2)}) %all-to-all-start) | async-done | bytes 917536 | tf_op jit(solution)/shard_map/all_to_all | solution.py:26
  59.6 146.3 %all-gather.3.cloned.1.call-done = bf16[3584,1792]{1,0:T(8,128)(2,1)} async-done(((bf16[448,1792]{1,0:T(8,128)(2,1)}), bf16[3584,1792]{1,0:T(8,128)(2,1)}) %all-gather.3.cloned.1.call-update) | async-done | bytes 12845072 | tf_op jit(solution)/shard_map/all_gather | solution.py:27
  205.9 6.8 convolution_convert_fusion
  216.0 10.6 %gather_fusion.1 = bf16[2048,1792]{1,0:T(8,128)(2,1)} fusion(bf16[128,1792]{1,0:T(8,128)(2,1)S(1)} %multiply_convert_fusion.1, s32[2048]{0:T(1024)S(1)} %get-tuple-element.5), kind=kCustom, calls=%fused_computation.1 | custom fusion | bytes 14688256 | tf_op jit(solution)/shard_map/gather | solution.py:56
  226.6 3.7 broadcast_select_fusion
  230.3 163.7 %all_to_all.35 = bf16[8,256,1792]{2,1,0:T(8,128)(2,1)S(1)} all-to-all(bf16[8,256,1792]{2,1,0:T(8,128)(2,1)S(1)} %broadcast_select_fusion), channel_id=1, replica_groups=mesh['dp'=2,'label'=8,'tensor'=2] {'label'}, dimensions={0} | all-to-all | bytes 14680064 | tf_op jit(solution)/shard_map/all_to_all | solution.py:62
  400.1 3.6 all-to-all-start.1
  403.7 6.5 all-to-all-done.1
  410.2 8.6 %all-reduce.3.cloned.1.call-done = bf16[8,2,128,256]{3,2,0,1:T(8,128)(2,1)} async-done(((bf16[8,2,128,256]{3,2,0,1:T(8,128)(2,1)}), bf16[8,2,128,256]{3,2,0,1:T(8,128)(2,1)}) %all-reduce.3.cloned.1.call-update) | async-done | bytes 1048592 | tf_op jit(solution)/shard_map/psum | solution.py:78
  418.9 4.0 convert_bitcast_fusion
  422.8 3.6 copy.30
  426.5 5.8 all-to-all-start.3
  432.5 160.9 %all-to-all-done.3 = bf16[8,256,1792]{2,1,0:T(8,128)(2,1)} async-done(((bf16[8,256,1792]{2,1,0:T(8,128)(2,1)}), bf16[8,256,1792]{2,1,0:T(8,128)(2,1)}, u32[]{:S(2)}, u32[]{:S(2)}) %all-to-all-start.3) | async-done | bytes 7340064 | tf_op jit(solution)/shard_map/all_to_all | solution.py:92
  593.4 12.0 %gather_fusion.2 = bf16[1024,1792]{1,0:T(8,128)(2,1)} fusion(bf16[2048,1792]{1,0:T(8,128)(2,1)} %bitcast.15, s32[1024]{0:T(1024)S(1)} %broadcast_clamp_fusion.1), kind=kCustom, calls=%fused_computation.2 | custom fusion | bytes 7344128 | tf_op jit(solution)/shard_map/gather | solution.py:99
  605.4 4.5 convert_reduce_fusion
  613.6 7.1 bitcast_convert_fusion
  620.8 58.7 %all-gather.5.cloned.1.call-done = bf16[1024,1792]{1,0:T(8,128)(2,1)} async-done(((bf16[128,1792]{1,0:T(8,128)(2,1)}), bf16[1024,1792]{1,0:T(8,128)(2,1)}) %all-gather.5.cloned.1.call-update) | async-done | bytes 3670032 | tf_op jit(solution)/shard_map/all_gather | solution.py:116
  679.5 5.0 fusion.6
  684.6 25.2 %reduce-scatter.2.cloned.1.call-done = bf16[2,128,1792]{2,1,0:T(8,128)(2,1)} async-done(((bf16[2,256,1792]{2,1,0:T(8,128)(2,1)}), bf16[2,128,1792]{2,1,0:T(8,128)(2,1)}) %reduce-scatter.2.cloned.1.call-update) | async-done | bytes 917520 | tf_op jit(solution)/shard_map/reduce_scatter | solution.py:106
  712.4 52.3 %all-reduce.5.cloned.1.call-done = bf16[448,1792]{1,0:T(8,128)(2,1)} async-done(((bf16[448,1792]{1,0:T(8,128)(2,1)}), bf16[448,1792]{1,0:T(8,128)(2,1)}) %all-reduce.5.cloned.1.call-update) | async-done | bytes 1605648 | tf_op jit(solution)/shard_map/psum | solution.py:120
  (66 shorter events, 23.3 us)
Async XLA Ops:
  7.2 389.8 %copy-start = (bf16[2,256,1792]{2,1,0:T(8,128)(2,1)S(1)}, bf16[2,256,1792]{2,1,0:T(8,128)(2,1)}, u32[]{:S(2)}) copy-start(bf16[2,256,1792]{2,1,0:T(8,128)(2,1)} %param.10) | copy-start | bytes 5505028
  7.2 1.3 copy-start.4
  7.2 198.7 %all-gather.3.cloned.1.call-start = ((), (), s32[]{:S(2)}) async-start(), calls=%async_computation.5 | async-start | bytes 14450688 | tf_op jit(solution)/shard_map/all_gather | solution.py:27
  8.5 8.4 %copy-start.7 = (s32[128,8]{0,1:T(8,128)S(1)}, s32[128,8]{0,1:T(8,128)}, u32[]{:S(2)}) copy-start(s32[128,8]{0,1:T(8,128)} %param.12) | copy-start | bytes 12292
  8.5 18.3 %copy-start.2 = (s32[128,2]{0,1:T(2,128)S(1)}, s32[128,2]{0,1:T(2,128)}, u32[]{:S(2)}) copy-start(s32[128,2]{0,1:T(2,128)} %param.13) | copy-start | bytes 3076
  9.6 50.1 %all-to-all-start = ((bf16[8,128,448]{1,2,0:T(8,128)(2,1)}), bf16[8,128,448]{1,2,0:T(8,128)(2,1)S(1)}, u32[]{:S(2)}, u32[]{:S(2)}) async-start(bf16[8,128,448]{1,2,0:T(8,128)(2,1)} %copy_bitcast_fusion), calls=%async_computation | async-start | bytes 1835008 | tf_op jit(solution)/shard_map/all_to_all | solution.py:26
  16.8 402.0 %all-reduce.3.cloned.1.call-start = ((), (), s32[]{:S(2)}) async-start(), calls=%async_computation.6 | async-start | bytes 2097152 | tf_op jit(solution)/shard_map/psum | solution.py:78
  212.7 3.1 copy-start.6
  394.0 3.0 copy-start.3
  397.0 6.7 copy-start.8
  400.1 10.2 %all-to-all-start.1 = ((s32[8,1,256]{2,1,0:T(1,128)}), s32[8,1,256]{2,1,0:T(1,128)S(1)}, u32[]{:S(2)}, u32[]{:S(2)}) async-start(s32[8,1,256]{2,1,0:T(1,128)} %bitcast.6), calls=%async_computation.1 | async-start | bytes 16384 | tf_op jit(solution)/shard_map/all_to_all | solution.py:69
  426.5 166.9 %all-to-all-start.3 = ((bf16[8,256,1792]{2,1,0:T(8,128)(2,1)}), bf16[8,256,1792]{2,1,0:T(8,128)(2,1)}, u32[]{:S(2)}, u32[]{:S(2)}) async-start(bf16[8,256,1792]{2,1,0:T(8,128)(2,1)} %bitcast.67), calls=%async_computation.3 | async-start | bytes 14680064 | tf_op jit(solution)/shard_map/all_to_all | solution.py:92
  432.3 247.2 %all-gather.5.cloned.1.call-start = ((), (), s32[]{:S(2)}) async-start(), calls=%async_computation.7 | async-start | bytes 4128768 | tf_op jit(solution)/shard_map/all_gather | solution.py:116
  613.5 66.0 %copy-start.5 = (bf16[1024,448]{0,1:T(8,128)(2,1)S(1)}, bf16[1024,448]{0,1:T(8,128)(2,1)}, u32[]{:S(2)}) copy-start(bf16[1024,448]{0,1:T(8,128)(2,1)} %param.7) | copy-start | bytes 2752516
  613.5 96.2 %reduce-scatter.2.cloned.1.call-start = ((), (), s32[]{:S(2)}) async-start(), calls=%async_computation.9 | async-start | bytes 2752512 | tf_op jit(solution)/shard_map/reduce_scatter | solution.py:106
  620.7 143.9 %all-reduce.5.cloned.1.call-start = ((), (), s32[]{:S(2)}) async-start(), calls=%async_computation.8 | async-start | bytes 3211264 | tf_op jit(solution)/shard_map/psum | solution.py:120
  709.7 58.3 %copy-start.1 = (bf16[2,256,1792]{2,1,0:T(8,128)(2,1)S(1)}, bf16[2,256,1792]{2,1,0:T(8,128)(2,1)}, u32[]{:S(2)}) copy-start(bf16[2,256,1792]{2,1,0:T(8,128)(2,1)} %param.10) | copy-start | bytes 5505028
Sparse Core Ops, SparseCore 0:
  10.2 195.6 all-gather.2
  400.2 18.6 all-reduce.2
  613.6 65.8 all-gather.4
  682.3 27.3 reduce-scatter.1
  712.4 52.1 all-reduce.4
where the time goes:
time: 775 us
  waiting for transfers between devices  475 us (61%)
  blocking collectives  169 us (22%)
  local copies, waits for them, and re-layouts  52.9 us (7%)
  matrix products  26 us (3%)
  other arithmetic  21.4 us (3%)
  starting transfers between devices  17.1 us (2%)
  between operations  14 us (2%)
    all_to_all x1, blocking collectives, shards(): lax.all_to_all(send_rows.reshape(labels_n, per_owner, width_half), 'label...  164 us
    all_to_all x1, waiting for transfers between devices, shards(): lax.all_to_all(back_terms.reshape(labels_n, per_owner, width_half), 'labe...  161 us
    all_gather x1, waiting for transfers between devices, shards(): shard_piece = lax.all_gather(enc_weight, 'label', axis=0, tiled=True)  146 us
    all_gather x1, waiting for transfers between devices, shards(): lax.all_gather(pooled_grad, 'label', axis=0, tiled=True)  58.7 us
    psum x1, waiting for transfers between devices, shards(): lax.psum(weight_part.astype(jnp.bfloat16), 'dp').astype(jnp.float32)  52.3 us
    reduce_scatter x1, waiting for transfers between devices, shards(): lax.psum_scatter(head_partial.astype(jnp.bfloat16), 'dp', scatter_dimensi...  25.2 us
    gather x1, local copies, waits for them, and re-layouts, shards(): offset_pick = offsets[src_row, jnp.minimum(src_slot, pos_count - 1)]  16.9 us
  transfers between devices with their start and end apart: 8, of which 8 were waited for; matrix products, arithmetic and copies ran while one was open for 6% of the time, Pallas kernels for 0%

commit v1 on v0

v1 whole, which is shorter than its diff:
```python
import jax
import jax.numpy as jnp
from jax import lax
from jax.sharding import PartitionSpec as P

EPSILON = 1e-06
F32 = jnp.float32
BF16 = jnp.bfloat16


def sum_over_dp(part):
    n = lax.axis_size("dp")
    if n == 2:
        other = lax.ppermute(part.astype(BF16), "dp", [(0, 1), (1, 0)])
        return part + other.astype(F32)
    return lax.psum(part.astype(BF16), "dp").astype(F32)


def scatter_over_dp(part):
    n = lax.axis_size("dp")
    if n == 2:
        half = part.shape[1] // 2
        me = lax.axis_index("dp")
        mine = lax.dynamic_slice_in_dim(part, me * half, half, 1)
        theirs = lax.dynamic_slice_in_dim(part, (1 - me) * half, half, 1)
        other = lax.ppermute(theirs.astype(BF16), "dp", [(0, 1), (1, 0)])
        return mine + other.astype(F32)
    return lax.psum_scatter(part.astype(BF16), "dp", scatter_dimension=1, tiled=True).astype(F32)


def shards(hidden, enc_weight, enc_gain, head_weight, propensity, blocks, offsets):
    width_half = enc_weight.shape[1]
    rows_here = blocks.shape[0]
    pos_count = offsets.shape[1]
    blocks_dev, block_size = head_weight.shape[:2]
    full_width = width_half * lax.axis_size("tensor")
    head = head_weight.reshape(blocks_dev * block_size, width_half)

    all_blocks = lax.all_gather(
        jnp.concatenate([blocks, offsets], axis=1), "label", axis=0, tiled=True
    )
    all_offsets = all_blocks[:, blocks.shape[1] :]
    all_blocks = all_blocks[:, : blocks.shape[1]]

    product = jnp.dot(hidden, enc_weight, preferred_element_type=F32).astype(BF16)
    pooled = lax.psum_scatter(product, "label", scatter_dimension=0, tiled=True).astype(F32)
    squares = lax.psum(jnp.sum(pooled * pooled, axis=1), "tensor")
    inverse = lax.rsqrt(squares / full_width + EPSILON)
    embedded = (pooled * inverse[:, None] * enc_gain[None, :]).astype(BF16)
    rows = lax.all_gather(embedded, "label", axis=0, tiled=True)

    partial = lax.dot_general(
        rows, head, (((1,), (1,)), ((), ())), preferred_element_type=F32
    )
    scores = lax.psum(partial.astype(BF16), "tensor").astype(F32)

    label_ids = jnp.arange(block_size, dtype=jnp.int32)[None, :]
    first = lax.axis_index("label") * blocks_dev
    pieces = []
    for n in range(blocks_dev):
        named = all_blocks == first + n
        present = jnp.any(named, axis=1)[:, None]
        positive = jnp.zeros((), bool)
        for k in range(pos_count):
            positive = positive | (
                named[:, k : k + 1] & (all_offsets[:, k : k + 1] == label_ids)
            )
        here = scores[:, n * block_size : (n + 1) * block_size]
        weight_pos = (1.0 / propensity[n])[None, :]
        above = jnp.maximum(1.0 - here, 0.0)
        below = jnp.maximum(1.0 + here, 0.0)
        slope = jnp.where(
            positive, -2.0 * weight_pos * above + 2.0 * (1.0 - weight_pos) * below, 2.0 * below
        )
        pieces.append(jnp.where(present, slope / rows_here, 0.0).astype(BF16))
    slopes = jnp.concatenate(pieces, axis=1)

    back = jnp.dot(slopes, head, preferred_element_type=F32).astype(BF16)
    embed_grad = lax.psum_scatter(back, "label", scatter_dimension=0, tiled=True).astype(F32)

    head_partial = lax.dot_general(
        slopes, rows, (((0,), (0,)), ((), ())), preferred_element_type=F32
    ).reshape(blocks_dev, block_size, width_half)
    head_grad = scatter_over_dp(head_partial)

    scaled = embed_grad * enc_gain[None, :]
    row_dot = lax.psum(jnp.sum(scaled * pooled, axis=1), "tensor")
    pooled_grad = (
        inverse[:, None] * (scaled - pooled * (inverse * inverse * row_dot / full_width)[:, None])
    ).astype(BF16)
    all_grad = lax.all_gather(pooled_grad, "label", axis=0, tiled=True)
    weight_part = lax.dot_general(
        hidden, all_grad, (((0,), (0,)), ((), ())), preferred_element_type=F32
    )
    enc_grad = sum_over_dp(weight_part)
    return (enc_grad, head_grad)


def solution(mesh):
    in_specs = (
        P("dp", "label"),
        P("label", "tensor"),
        P("tensor"),
        P("label", None, "tensor"),
        P("label", None),
        P(("dp", "label"), None),
        P(("dp", "label"), None),
    )
    out_specs = (P("label", "tensor"), P("label", "dp", "tensor"))
    return jax.shard_map(shards, mesh=mesh, in_specs=in_specs, out_specs=out_specs, check_vma=False)
```

time: 775 us -> 439 us (0.57)
  blocking collectives: 169 us -> 35.4 us
  waiting for transfers between devices: 475 us -> 342 us
  local copies, waits for them, and re-layouts: 52.9 us -> 2.61 us
  starting transfers between devices: 17.1 us -> 2.23 us
    all_to_all x3 -> x0, waiting for transfers between devices: 183 us -> none  [the longest x1 161 us: shards(): lax.all_to_all(back_terms.reshape(labels_n, per_owner, width_half), 'labe...]
    all_to_all x1 -> x0, blocking collectives: 164 us -> none  [shards(): lax.all_to_all(send_rows.reshape(labels_n, per_owner, width_half), 'label...]
    reduce_scatter x1 -> x2, waiting for transfers between devices: 25.2 us -> 163 us  [the longest x1 84 us: shards(): lax.psum_scatter(product, 'label', scatter_dimension=0, tiled=True)]
    all_gather x2, waiting for transfers between devices: 205 us -> 127 us  [the longest x1 66.6 us: shards(): rows = lax.all_gather(embedded, 'label', axis=0, tiled=True)]
    psum x2 -> x1, waiting for transfers between devices: 60.9 us -> 0.02 us  [shards(): scores = lax.psum(partial.astype(BF16), 'tensor').astype(F32)]
    ppermute x0 -> x2, waiting for transfers between devices: none -> 51.3 us  [the longest x1 51.3 us: scatter_over_dp(): other = lax.ppermute(theirs.astype(BF16), 'dp', [(0, 1), (1, 0)])]
    gather x3 -> x0, local copies, waits for them, and re-layouts: 39.5 us -> none  [the longest x1 16.9 us: shards(): offset_pick = offsets[src_row, jnp.minimum(src_slot, pos_count - 1)]]
    all_gather x0 -> x1, blocking collectives: none -> 30.5 us  [shards(): lax.all_gather(jnp.concatenate([blocks, offsets], axis=1), 'label', axis=...]
  transfers between devices with their start and end apart: 8 -> 7, of which waited for: 8 -> 5; matrix products, arithmetic and copies ran while one was open for 6% -> 3% of each run, Pallas kernels for 0% -> 0%
where the time goes in v1:
time: 439 us; the launch traced here: 438 us
  waiting for transfers between devices  342 us (78%)
  blocking collectives  35.4 us (8%)
  matrix products  27.1 us (6%)
  other arithmetic  15.1 us (3%)
  between operations  13.9 us (3%)
    reduce_scatter x1, waiting for transfers between devices, shards(): lax.psum_scatter(product, 'label', scatter_dimension=0, tiled=True)  84 us
    reduce_scatter x1, waiting for transfers between devices, shards(): lax.psum_scatter(back, 'label', scatter_dimension=0, tiled=True).astype(F32)  79.3 us
    all_gather x1, waiting for transfers between devices, shards(): rows = lax.all_gather(embedded, 'label', axis=0, tiled=True)  66.6 us
    all_gather x1, waiting for transfers between devices, shards(): all_grad = lax.all_gather(pooled_grad, 'label', axis=0, tiled=True)  60.7 us
    ppermute x1, waiting for transfers between devices, scatter_over_dp(): other = lax.ppermute(theirs.astype(BF16), 'dp', [(0, 1), (1, 0)])  51.3 us
    all_gather x1, blocking collectives, shards(): lax.all_gather(jnp.concatenate([blocks, offsets], axis=1), 'label', axis=...  30.5 us
  transfers between devices with their start and end apart: 7, of which 5 were waited for; matrix products, arithmetic and copies ran while one was open for 3% of the time, Pallas kernels for 0%

profile of v1, /device:TPU:0, one launch (start us, length us, event | category | flops | bytes accessed | tf_op | source)
XLA Modules:
  0.0 438.3 jit_solution(1559239294848319680)
XLA Ops:
  7.2 5.7 %convolution_convert_fusion.1 = bf16[1024,1792]{1,0:T(8,128)(2,1)} fusion(bf16[1024,448]{0,1:T(8,128)(2,1)} %param.7, bf16[448,1792]{1,0:T(8,128)(2,1)} %param.8), kind=kOutput, calls=%fused_computation.1 | convolution fusion | flops 1646002176 | bytes 6193152 | tf_op jit(solution)/shard_map/dot_general | solution.py:45
  13.0 84.0 %reduce-scatter.3.cloned.1.call-done = bf16[128,1792]{1,0:T(8,128)(2,1)} async-done(((bf16[1024,1792]{1,0:T(8,128)(2,1)}), bf16[128,1792]{1,0:T(8,128)(2,1)}) %reduce-scatter.3.cloned.1.call-update) | async-done | bytes 458768 | tf_op jit(solution)/shard_map/reduce_scatter | solution.py:46
  97.1 1.2 fusion.6
  98.3 2.5 psum.21
  100.7 2.0 fusion.8
  102.8 66.6 %all-gather.3.cloned.1.call-done = bf16[1024,1792]{1,0:T(8,128)(2,1)} async-done(((bf16[128,1792]{1,0:T(8,128)(2,1)}), bf16[1024,1792]{1,0:T(8,128)(2,1)}) %all-gather.3.cloned.1.call-update) | async-done | bytes 3670032 | tf_op jit(solution)/shard_map/all_gather | solution.py:50
  169.4 5.1 %convolution_convert_fusion.2 = bf16[1024,512]{1,0:T(8,128)(2,1)} fusion(bf16[1024,1792]{1,0:T(8,128)(2,1)} %all-gather.3.cloned.1.call-done, bf16[512,1792]{1,0:T(8,128)(2,1)S(1)} %bitcast.19), kind=kOutput, calls=%fused_computation.10 | convolution fusion | flops 1879572480 | bytes 6553600 | tf_op jit(solution)/shard_map/dot_general | solution.py:52
  174.6 30.5 %all_gather.9 = s32[1024,10]{0,1:T(8,128)S(1)} all-gather(s32[128,10]{0,1:T(8,128)S(1)} %pad_add_fusion), channel_id=1, replica_groups=mesh['dp'=2,'label'=8,'tensor'=2] {'label'}, dimensions={0}, use_global_device_ids=true | all-gather | bytes 46080 | tf_op jit(solution)/shard_map/all_gather | solution.py:39
  205.3 1.5 convert_element_type.46
  206.8 1.8 select_convert_fusion.1
  208.7 3.9 convolution_convert_fusion
  212.6 79.3 %reduce-scatter.5.cloned.1.call-done = bf16[128,1792]{1,0:T(8,128)(2,1)} async-done(((bf16[1024,1792]{1,0:T(8,128)(2,1)}), bf16[128,1792]{1,0:T(8,128)(2,1)}) %reduce-scatter.5.cloned.1.call-update) | async-done | bytes 458768 | tf_op jit(solution)/shard_map/reduce_scatter | solution.py:79
  291.9 1.3 fusion.9
  293.2 2.5 psum.23
  295.7 2.1 fusion.12
  297.8 6.0 %fusion.13 = f32[512,1792]{1,0:T(8,128)} fusion(bf16[1024,1792]{1,0:T(8,128)(2,1)} %all-gather.3.cloned.1.call-done, bf16[1024,256]{1,0:T(8,128)(2,1)S(1)} %get-tuple-element.15, bf16[1024,256]{1,0:T(8,128)(2,1)S(1)} %get-tuple-element.14), kind=kOutput, calls=%fused_computation.30 | convolution fusion | flops 1881145344 | bytes 8388608 | tf_op jit(solution)/shard_map/dot_general | solution.py:81
  303.8 60.7 %all-gather.5.cloned.1.call-done = bf16[1024,1792]{1,0:T(8,128)(2,1)} async-done(((bf16[128,1792]{1,0:T(8,128)(2,1)}), bf16[1024,1792]{1,0:T(8,128)(2,1)}) %all-gather.5.cloned.1.call-update) | async-done | bytes 3670032 | tf_op jit(solution)/shard_map/all_gather | solution.py:91
  364.5 6.4 %bitcast_convert_fusion = (bf16[448,1792]{1,0:T(8,128)(2,1)}, f32[1792,448]{0,1:T(8,128)}) fusion(bf16[1024,448]{0,1:T(8,128)(2,1)} %param.7, bf16[1024,1792]{1,0:T(8,128)(2,1)} %all-gather.5.cloned.1.call-done), kind=kOutput, calls=%fused_computation.3 | convolution fusion | flops 1644969984 | bytes 9404416 | tf_op jit(solution)/shard_map/dot_general | solution.py:92
  370.8 1.5 collective-permute-start
  372.3 2.5 dynamic-slice_convert_fusion
  374.8 0.6 collective-permute-start.1
  375.4 51.3 %collective-permute-done.1 = bf16[2,128,1792]{2,1,0:T(8,128)(2,1)} collective-permute-done((bf16[2,128,1792]{2,1,0:T(8,128)(2,1)}, bf16[2,128,1792]{2,1,0:T(8,128)(2,1)}, u32[]{:S(2)}, u32[]{:S(2)}) %collective-permute-start.1) | collective-permute-done | bytes 917536 | tf_op jit(solution)/shard_map/ppermute | solution.py:26
  426.7 3.2 convert_add_fusion
  429.8 2.0 bitcast_add_fusion
  (34 shorter events, 0.5 us)
Async XLA Ops:
  7.2 162.2 %copy-start = (bf16[2,256,1792]{2,1,0:T(8,128)(2,1)S(1)}, bf16[2,256,1792]{2,1,0:T(8,128)(2,1)}, u32[]{:S(2)}) copy-start(bf16[2,256,1792]{2,1,0:T(8,128)(2,1)} %param.10) | copy-start | bytes 5505028
  7.2 89.9 %reduce-scatter.3.cloned.1.call-start = ((), (), s32[]{:S(2)}) async-start(), calls=%async_computation.2 | async-start | bytes 4128768 | tf_op jit(solution)/shard_map/reduce_scatter | solution.py:46
  13.0 87.8 %copy-start.3 = (f32[1792]{0:T(1024)S(1)}, f32[1792]{0:T(1024)}, u32[]{:S(2)}) copy-start(f32[1792]{0:T(1024)} %param.9) | copy-start | bytes 21508
  13.0 156.4 %all-gather.3.cloned.1.call-start = ((), (), s32[]{:S(2)}) async-start(), calls=%async_computation.3 | async-start | bytes 4128768 | tf_op jit(solution)/shard_map/all_gather | solution.py:50
  102.7 102.6 %all-reduce.2.cloned.1.call-start = ((), (), s32[]{:S(2)}) async-start(), calls=%async_computation.4 | async-start | bytes 2097152 | tf_op jit(solution)/shard_map/psum | solution.py:55
  169.4 5.2 %copy-start.4 = (s32[128,8]{0,1:T(8,128)S(1)}, s32[128,8]{0,1:T(8,128)}, u32[]{:S(2)}) copy-start(s32[128,8]{0,1:T(8,128)} %param.12) | copy-start | bytes 12292
  169.4 5.2 %copy-start.6 = (s32[128,2]{0,1:T(2,128)S(1)}, s32[128,2]{0,1:T(2,128)}, u32[]{:S(2)}) copy-start(s32[128,2]{0,1:T(2,128)} %param.13) | copy-start | bytes 3076
  169.4 35.8 %copy-start.5 = (f32[2,256]{1,0:T(2,128)S(1)}, f32[2,256]{1,0:T(2,128)}, u32[]{:S(2)}) copy-start(f32[2,256]{1,0:T(2,128)} %param.11) | copy-start | bytes 6148
  174.5 117.4 %reduce-scatter.5.cloned.1.call-start = ((), (), s32[]{:S(2)}) async-start(), calls=%async_computation.5 | async-start | bytes 4128768 | tf_op jit(solution)/shard_map/reduce_scatter | solution.py:79
  212.6 79.4 %copy-start.1 = (bf16[128,1792]{1,0:T(8,128)(2,1)S(1)}, bf16[128,1792]{1,0:T(8,128)(2,1)}, u32[]{:S(2)}) copy-start(bf16[128,1792]{1,0:T(8,128)(2,1)} %reduce-scatter.3.cloned.1.call-done) | copy-start | bytes 1376260
  212.6 151.9 %all-gather.5.cloned.1.call-start = ((), (), s32[]{:S(2)}) async-start(), calls=%async_computation.6 | async-start | bytes 4128768 | tf_op jit(solution)/shard_map/all_gather | solution.py:91
  370.8 59.0 %collective-permute-start = (bf16[448,1792]{1,0:T(8,128)(2,1)}, bf16[448,1792]{1,0:T(8,128)(2,1)S(1)}, u32[]{:S(2)}, u32[]{:S(2)}) collective-permute-start(bf16[448,1792]{1,0:T(8,128)(2,1)} %get-tuple-element.22), channel_id=1, source_target_pairs={{0,16},{16,0},{1,17},{17,1},{2,18},{18,2},{3,19},{19,3},{4,20},{20... | collective-permute-start | bytes 4816904 | tf_op jit(solution)/shard_map/ppermute | solution.py:14
  374.8 51.8 %collective-permute-start.1 = (bf16[2,128,1792]{2,1,0:T(8,128)(2,1)}, bf16[2,128,1792]{2,1,0:T(8,128)(2,1)}, u32[]{:S(2)}, u32[]{:S(2)}) collective-permute-start(bf16[2,128,1792]{2,1,0:T(8,128)(2,1)} %dynamic-slice_convert_fusion), channel_id=1, source_target_pairs={{0,16},{16,0},{1,17},{17,1},{2,18},{18,2},{3,19},{19,3},{4,20},{20... | collective-permute-start | bytes 2752520 | tf_op jit(solution)/shard_map/ppermute | solution.py:26
  375.4 54.4 %copy-start.2 = (f32[1792,448]{0,1:T(8,128)S(1)}, f32[1792,448]{0,1:T(8,128)}, u32[]{:S(2)}) copy-start(f32[1792,448]{0,1:T(8,128)} %get-tuple-element.23) | copy-start | bytes 9633796
Sparse Core Ops, SparseCore 0:
  13.1 83.9 reduce-scatter.2
  102.9 66.4 all-gather.2
  174.7 18.0 all-reduce.1
  212.7 79.1 reduce-scatter.4
  297.9 66.5 all-gather.4

commit v2 on v1

--- a/solution.py
+++ b/solution.py
@@ -1,11 +1,261 @@
+import functools
+
 import jax
 import jax.numpy as jnp
 from jax import lax
+from jax.experimental import pallas as pl
+from jax.experimental.pallas import tpu as pltpu
 from jax.sharding import PartitionSpec as P
 
 EPSILON = 1e-06
 F32 = jnp.float32
 BF16 = jnp.bfloat16
+
+
+MESH = pl.DeviceIdType.MESH
+FAST = 2
+VMEM_LIMIT = 40 * 1024 * 1024
+
+
+def spot():
+    me = lax.axis_index("label")
+    return me // FAST, lax.rem(me, FAST)
+
+
+def at(axis, index):
+    here = {name: lax.axis_index(name) for name in ("dp", "label", "tensor")}
+    here[axis] = index
+    return (here["dp"], here["label"], here["tensor"])
+
+
+def greet(devices):
+    barrier = pltpu.get_barrier_semaphore()
+    for device in devices:
+        pl.semaphore_signal(barrier, inc=1, device_id=device, device_id_type=MESH)
+    pl.semaphore_wait(barrier, len(devices))
+
+
+def neighbours(high, low, z, length):
+    found = [at("label", z * FAST + 1 - low)]
+    if z + 1 < length:
+        found.append(at("label", (z + 1) * FAST + low))
+    if z > 0:
+        found.append(at("label", (z - 1) * FAST + low))
+    return found
+
+
+def gather_kernel(length, count, *refs):
+    sources, gathered = refs[:count], refs[count : 2 * count]
+    send_sem, recv_sem = refs[2 * count :]
+    high, low = spot()
+
+    def copies(way, block, first, device):
+        return [
+            pltpu.make_async_remote_copy(
+                src_ref=sources[i] if first else gathered[i].at[block],
+                dst_ref=gathered[i].at[block],
+                send_sem=send_sem.at[i, way, block],
+                recv_sem=recv_sem.at[i, block],
+                device_id=device,
+                device_id_type=MESH,
+            )
+            for i in range(count)
+        ]
+
+    def branch(z):
+        across = at("label", z * FAST + 1 - low)
+        up = at("label", (z + 1) * FAST + low)
+        down = at("label", (z - 1) * FAST + low)
+        greet(neighbours(high, low, z, length))
+        sent = []
+
+        def send(way, block, first, device):
+            made = copies(way, block, first, device)
+            for copy in made:
+                copy.start()
+            sent.extend(made)
+
+        def arrived(block):
+            for copy in copies(0, block, False, across):
+                copy.wait_recv()
+
+        own = z * FAST + low
+        if z + 1 < length:
+            send(1, own, True, up)
+        if z > 0:
+            send(2, own, True, down)
+        send(0, own, True, across)
+        for i in range(count):
+            gathered[i][own] = sources[i][...]
+        for step in range(1, length):
+            if z - step >= 0:
+                block = (z - step) * FAST + low
+                arrived(block)
+                if z + 1 < length:
+                    send(1, block, False, up)
+                send(0, block, False, across)
+            if z + step < length:
+                block = (z + step) * FAST + low
+                arrived(block)
+                if z > 0:
+                    send(2, block, False, down)
+                send(0, block, False, across)
+        for other in sorted(range(length), key=lambda t: abs(t - z)):
+            arrived(other * FAST + 1 - low)
+        for copy in sent:
+            copy.wait_send()
+
+    for z in range(length):
+        pl.when(high == z)(functools.partial(branch, z))
+
+
+def gather_label(arrays, number):
+    devices = lax.axis_size("label")
+    if devices != 4 * FAST:
+        return [lax.all_gather(a, "label", axis=0) for a in arrays]
+    count = len(arrays)
+    return pl.pallas_call(
+        functools.partial(gather_kernel, devices // FAST, count),
+        out_shape=[jax.ShapeDtypeStruct((devices,) + a.shape, a.dtype) for a in arrays],
+        in_specs=[pl.BlockSpec(memory_space=pltpu.VMEM)] * count,
+        out_specs=[pl.BlockSpec(memory_space=pltpu.VMEM)] * count,
+        scratch_shapes=[
+            pltpu.SemaphoreType.DMA((count, 3, devices)),
+            pltpu.SemaphoreType.DMA((count, devices)),
+        ],
+        compiler_params=pltpu.CompilerParams(
+            collective_id=number, has_side_effects=True, vmem_limit_bytes=VMEM_LIMIT
+        ),
+    )(*arrays)
+
+
+def scatter_kernel(length, swap, *refs):
+    if swap:
+        parts, theirs, out, other = refs[:4]
+        rest = refs[4:]
+    else:
+        parts, out = refs[:2]
+        rest = refs[2:]
+    crossed, in_up, in_down, out_up, out_down, send_sem, recv_sem, swap_sem = rest
+    high, low = spot()
+    rows = parts.shape[1]
+    tile = 16
+
+    def remote(src, dst, way, t, device):
+        return pltpu.make_async_remote_copy(
+            src_ref=src,
+            dst_ref=dst,
+            send_sem=send_sem.at[way, t],
+            recv_sem=recv_sem.at[way, t],
+            device_id=device,
+            device_id_type=MESH,
+        )
+
+    def branch(z):
+        across = at("label", z * FAST + 1 - low)
+        up = at("label", (z + 1) * FAST + low)
+        down = at("label", (z - 1) * FAST + low)
+        greeted = neighbours(high, low, z, length)
+        if swap:
+            beside = at("dp", 1 - lax.axis_index("dp"))
+            greeted.append(beside)
+        greet(greeted)
+        sent = []
+        if swap:
+            exchange = pltpu.make_async_remote_copy(
+                src_ref=theirs,
+                dst_ref=other,
+                send_sem=swap_sem.at[0],
+                recv_sem=swap_sem.at[1],
+                device_id=beside,
+                device_id_type=MESH,
+            )
+            exchange.start()
+
+        order = sorted(range(length), key=lambda t: (-abs(t - z), -t))
+
+        def cross(t):
+            copy = remote(parts.at[t * FAST + 1 - low], crossed.at[t], 0, t, across)
+            copy.start()
+            sent.append(copy)
+
+        def total(t, terms, result):
+            def body(i, carry):
+                span = pl.ds(pl.multiple_of(i * tile, tile), tile)
+                value = parts[t * FAST + low, span].astype(F32) + crossed[t, span].astype(F32)
+                for term in terms:
+                    value += term[t, span].astype(F32)
+                if result is None:
+                    out[span] = value
+                else:
+                    result[t, span] = value.astype(BF16)
+                return carry
+
+            lax.fori_loop(0, rows // tile, body, 0)
+
+        for t in order[:2]:
+            cross(t)
+        for place, t in enumerate(order):
+            remote(parts.at[0], crossed.at[t], 0, t, across).wait_recv()
+            if place + 2 < length:
+                cross(order[place + 2])
+            terms = []
+            if t >= z and z > 0:
+                remote(out_up.at[t], in_up.at[t], 1, t, across).wait_recv()
+                terms.append(in_up)
+            if t <= z and z + 1 < length:
+                remote(out_down.at[t], in_down.at[t], 2, t, across).wait_recv()
+                terms.append(in_down)
+            if t > z:
+                total(t, terms, out_up)
+                copy = remote(out_up.at[t], in_up.at[t], 1, t, up)
+            elif t < z:
+                total(t, terms, out_down)
+                copy = remote(out_down.at[t], in_down.at[t], 2, t, down)
+            else:
+                total(t, terms, None)
+                continue
+            copy.start()
+            sent.append(copy)
+        for copy in sent:
+            copy.wait_send()
+        if swap:
+            exchange.wait()
+
+    for z in range(length):
+        pl.when(high == z)(functools.partial(branch, z))
+
+
+def scatter_label(parts, number, theirs=None):
+    devices, rows, width = parts.shape
+    swap = theirs is not None
+    if devices != 4 * FAST:
+        out = lax.psum_scatter(parts, "label", scatter_dimension=0, tiled=False).astype(F32)
+        if swap:
+            return out, lax.ppermute(theirs, "dp", [(0, 1), (1, 0)])
+        return out
+    length = devices // FAST
+    out_shape = [jax.ShapeDtypeStruct((rows, width), F32)]
+    operands = [parts]
+    if swap:
+        out_shape.append(jax.ShapeDtypeStruct(theirs.shape, theirs.dtype))
+        operands.append(theirs)
+    outs = pl.pallas_call(
+        functools.partial(scatter_kernel, length, swap),
+        out_shape=out_shape,
+        in_specs=[pl.BlockSpec(memory_space=pltpu.VMEM)] * len(operands),
+        out_specs=[pl.BlockSpec(memory_space=pltpu.VMEM)] * len(operands),
+        scratch_shapes=[pltpu.VMEM((length, rows, width), BF16)] * 5
+        + [
+            pltpu.SemaphoreType.DMA((3, length)),
+            pltpu.SemaphoreType.DMA((3, length)),
+            pltpu.SemaphoreType.DMA((2,)),
+        ],
+        compiler_params=pltpu.CompilerParams(
+            collective_id=number, has_side_effects=True, vmem_limit_bytes=VMEM_LIMIT
+        ),
+    )(*operands)
+    return outs if swap else outs[0]
 
 
 def sum_over_dp(part):
@@ -14,18 +264,6 @@
         other = lax.ppermute(part.astype(BF16), "dp", [(0, 1), (1, 0)])
         return part + other.astype(F32)
     return lax.psum(part.astype(BF16), "dp").astype(F32)
-
-
-def scatter_over_dp(part):
-    n = lax.axis_size("dp")
-    if n == 2:
-        half = part.shape[1] // 2
-        me = lax.axis_index("dp")
-        mine = lax.dynamic_slice_in_dim(part, me * half, half, 1)
-        theirs = lax.dynamic_slice_in_dim(part, (1 - me) * half, half, 1)
-        other = lax.ppermute(theirs.astype(BF16), "dp", [(0, 1), (1, 0)])
-        return mine + other.astype(F32)
-    return lax.psum_scatter(part.astype(BF16), "dp", scatter_dimension=1, tiled=True).astype(F32)
 
 
 def shards(hidden, enc_weight, enc_gain, head_weight, propensity, blocks, offsets):
@@ -36,18 +274,20 @@
     full_width = width_half * lax.axis_size("tensor")
     head = head_weight.reshape(blocks_dev * block_size, width_half)
 
-    all_blocks = lax.all_gather(
-        jnp.concatenate([blocks, offsets], axis=1), "label", axis=0, tiled=True
-    )
-    all_offsets = all_blocks[:, blocks.shape[1] :]
-    all_blocks = all_blocks[:, : blocks.shape[1]]
+    labels_n = lax.axis_size("label")
+    slots = blocks.shape[1]
+    targets = jnp.concatenate([blocks, offsets], axis=1).T
+    targets = jnp.pad(targets, ((0, -targets.shape[0] % 8), (0, 0)))
 
     product = jnp.dot(hidden, enc_weight, preferred_element_type=F32).astype(BF16)
-    pooled = lax.psum_scatter(product, "label", scatter_dimension=0, tiled=True).astype(F32)
+    pooled = scatter_label(product.reshape(labels_n, rows_here, width_half), 0)
     squares = lax.psum(jnp.sum(pooled * pooled, axis=1), "tensor")
     inverse = lax.rsqrt(squares / full_width + EPSILON)
     embedded = (pooled * inverse[:, None] * enc_gain[None, :]).astype(BF16)
-    rows = lax.all_gather(embedded, "label", axis=0, tiled=True)
+    rows, targets = gather_label([embedded, targets], 1)
+    rows = rows.reshape(labels_n * rows_here, width_half)
+    targets = jnp.swapaxes(targets, 1, 2).reshape(labels_n * rows_here, -1)
+    all_blocks, all_offsets = targets[:, :slots], targets[:, slots : slots + pos_count]
 
     partial = lax.dot_general(
         rows, head, (((1,), (1,)), ((), ())), preferred_element_type=F32
@@ -76,19 +316,30 @@
     slopes = jnp.concatenate(pieces, axis=1)
 
     back = jnp.dot(slopes, head, preferred_element_type=F32).astype(BF16)
-    embed_grad = lax.psum_scatter(back, "label", scatter_dimension=0, tiled=True).astype(F32)
-
+    back = back.reshape(labels_n, rows_here, width_half)
     head_partial = lax.dot_general(
         slopes, rows, (((0,), (0,)), ((), ())), preferred_element_type=F32
     ).reshape(blocks_dev, block_size, width_half)
-    head_grad = scatter_over_dp(head_partial)
+    if lax.axis_size("dp") == 2:
+        half = block_size // 2
+        me = lax.axis_index("dp")
+        mine = lax.dynamic_slice_in_dim(head_partial, me * half, half, 1)
+        theirs = lax.dynamic_slice_in_dim(head_partial, (1 - me) * half, half, 1)
+        embed_grad, other = scatter_label(back, 2, theirs.astype(BF16))
+        head_grad = mine + other.astype(F32)
+    else:
+        embed_grad = scatter_label(back, 2)
+        head_grad = lax.psum_scatter(
+            head_partial.astype(BF16), "dp", scatter_dimension=1, tiled=True
+        ).astype(F32)
 
     scaled = embed_grad * enc_gain[None, :]
     row_dot = lax.psum(jnp.sum(scaled * pooled, axis=1), "tensor")
     pooled_grad = (
         inverse[:, None] * (scaled - pooled * (inverse * inverse * row_dot / full_width)[:, None])
     ).astype(BF16)
-    all_grad = lax.all_gather(pooled_grad, "label", axis=0, tiled=True)
+    (all_grad,) = gather_label([pooled_grad], 3)
+    all_grad = all_grad.reshape(labels_n * rows_here, width_half)
     weight_part = lax.dot_general(
         hidden, all_grad, (((0,), (0,)), ((), ())), preferred_element_type=F32
     )

time: 439 us -> 293 us (0.67)
  waiting for transfers between devices: 342 us -> 49.3 us
  Pallas kernels: 0 us -> 183 us
  blocking collectives: 35.4 us -> 4.92 us
  matrix products: 27.1 us -> 19.5 us
  local copies, waits for them, and re-layouts: 2.61 us -> 7.8 us
    pallas_call x0 -> x4, Pallas kernels: none -> 183 us  [the longest x2 92.9 us: scatter_label(): pl.pallas_call(functools.partial(scatter_kernel, length, swap), out_shape...]
    reduce_scatter x2 -> x0, waiting for transfers between devices: 163 us -> none  [the longest x1 84 us: shards(): lax.psum_scatter(product, 'label', scatter_dimension=0, tiled=True)]
    all_gather x2 -> x0, waiting for transfers between devices: 127 us -> none  [the longest x1 66.6 us: shards(): rows = lax.all_gather(embedded, 'label', axis=0, tiled=True)]
    ppermute x1 -> x0, waiting for transfers between devices: 51.3 us -> none  [scatter_over_dp(): other = lax.ppermute(theirs.astype(BF16), 'dp', [(0, 1), (1, 0)])]
    ppermute x1, waiting for transfers between devices: 0.01 us -> 30.6 us  [sum_over_dp(): other = lax.ppermute(part.astype(BF16), 'dp', [(0, 1), (1, 0)])]
    all_gather x1 -> x0, blocking collectives: 30.5 us -> none  [shards(): lax.all_gather(jnp.concatenate([blocks, offsets], axis=1), 'label', axis=...]
    psum x1, waiting for transfers between devices: 0.02 us -> 18.6 us  [shards(): scores = lax.psum(partial.astype(BF16), 'tensor').astype(F32)]
    unnamed x14 -> x26, local copies, waits for them, and re-layouts: 0.03 us -> 5.36 us
  transfers between devices with their start and end apart: 7 -> 2, of which waited for: 5 -> 2; matrix products, arithmetic and copies ran while one was open for 3% -> 1% of each run, Pallas kernels for 0% -> 0%
where the time goes in v2:
time: 293 us
  Pallas kernels  183 us (62%)
  waiting for transfers between devices  49.3 us (17%)
  matrix products  19.5 us (7%)
  between operations  14.3 us (5%)
  other arithmetic  12.7 us (4%)
  local copies, waits for them, and re-layouts  7.8 us (3%)
  blocking collectives  4.92 us (2%)
    pallas_call x2, Pallas kernels, scatter_label(): pl.pallas_call(functools.partial(scatter_kernel, length, swap), out_shape...  92.9 us
    pallas_call x2, Pallas kernels, gather_label(): pl.pallas_call(functools.partial(gather_kernel, devices // FAST, count),...  90.3 us
    ppermute x1, waiting for transfers between devices, sum_over_dp(): other = lax.ppermute(part.astype(BF16), 'dp', [(0, 1), (1, 0)])  30.6 us
    psum x1, waiting for transfers between devices, shards(): scores = lax.psum(partial.astype(BF16), 'tensor').astype(F32)  18.6 us
  transfers between devices with their start and end apart: 2, of which 2 were waited for; matrix products, arithmetic and copies ran while one was open for 1% of the time, Pallas kernels for 0%

profile of v2, /device:TPU:0, one launch (start us, length us, event | category | flops | bytes accessed | tf_op | source)
XLA Modules:
  0.0 293.0 jit_solution(7549529350047044124)
XLA Ops:
  7.2 3.9 %convolution_convert_fusion.1 = bf16[1024,1792]{1,0:T(8,128)(2,1)S(1)} fusion(bf16[1024,448]{0,1:T(8,128)(2,1)} %param.7, bf16[448,1792]{1,0:T(8,128)(2,1)} %param.8), kind=kOutput, calls=%fused_computation.1 | convolution fusion | flops 1646002176 | bytes 6193152 | tf_op jit(solution)/shard_map/dot_general | solution.py:282
  11.2 46.4 %shard_map.86 = f32[128,1792]{1,0:T(8,128)S(1)} custom-call(bf16[8,128,1792]{2,1,0:T(8,128)(2,1)S(1)} %bitcast.40), custom_call_target="tpu_custom_call" | custom-call | tf_op jit(solution)/shard_map/pallas_call | solution.py:243
  57.7 2.5 psum.21
  60.4 45.8 %shard_map.87 = (bf16[8,128,1792]{2,1,0:T(8,128)(2,1)S(1)}, s32[8,16,128]{2,1,0:T(8,128)S(1)}) custom-call(bf16[128,1792]{1,0:T(8,128)(2,1)S(1)} %multiply_convert_fusion.1.refs_0_, s32[16,128]{1,0:T(8,128)S(1)} %pad.4.refs_1_), custom_call_target="tpu_custom_call" | custom-call | tf_op jit(solution)/shard_map/pallas_call | solution.py:117
  106.2 1.8 copy-done.5
  108.0 3.1 %convolution_convert_fusion.2 = bf16[1024,512]{1,0:T(8,128)(2,1)} fusion(bf16[1024,1792]{1,0:T(8,128)(2,1)S(1)} %bitcast.41, bf16[512,1792]{1,0:T(8,128)(2,1)S(1)} %bitcast.36), kind=kOutput, calls=%fused_computation.6 | convolution fusion | flops 1879572480 | bytes 6553600 | tf_op jit(solution)/shard_map/dot_general | solution.py:292
  111.2 18.6 %all-reduce.3.cloned.1.call-done = bf16[1024,512]{1,0:T(8,128)(2,1)} async-done(((bf16[1024,512]{1,0:T(8,128)(2,1)}), bf16[1024,512]{1,0:T(8,128)(2,1)}) %all-reduce.3.cloned.1.call-update) | async-done | bytes 1048592 | tf_op jit(solution)/shard_map/psum | solution.py:295
  129.9 1.5 convert_element_type.39
  131.4 1.8 select_convert_fusion.1
  133.2 1.1 fusion.6
  134.3 3.9 %convolution_convert_fusion = bf16[1024,1792]{1,0:T(8,128)(2,1)} fusion(bf16[512,1792]{1,0:T(8,128)(2,1)S(1)} %bitcast.37, bf16[1024,256]{1,0:T(8,128)(2,1)S(1)} %get-tuple-element.23, bf16[1024,256]{1,0:T(8,128)(2,1)S(1)} %get-tuple-element.22), kind=kOutput, calls=%fused_computation | convolution fusion | flops 1882980352 | bytes 6553600 | tf_op jit(solution)/shard_map/dot_general | solution.py:318
  138.2 2.3 copy.12
  140.4 4.6 %fusion.11 = f32[2,256,1792]{2,1,0:T(8,128)S(1)} fusion(bf16[2,256,1024]{2,1,0:T(8,128)(2,1)} %bitcast.43, bf16[1024,1792,1]{1,0,2:T(8,128)(2,1)} %bitcast.42), kind=kOutput, calls=%fused_computation.43 | convolution fusion | flops 1879048192 | bytes 8388608 | tf_op jit(solution)/shard_map/dot_general | solution.py:320
  145.1 1.7 copy-done.7
  146.8 46.6 %shard_map.88 = (f32[128,1792]{1,0:T(8,128)S(1)}, bf16[2,128,1792]{2,1,0:T(8,128)(2,1)S(1)}) custom-call(bf16[8,128,1792]{2,1,0:T(8,128)(2,1)S(1)} %bitcast.38, bf16[2,128,1792]{2,1,0:T(8,128)(2,1)S(1)} %dynamic-slice_convert_fusion.refs_1_), custom_call_target="tpu_custom_call" | custom-call | tf_op jit(solution)/shard_map/pallas_call | solution.py:243
  194.3 0.9 copy-done.2
  195.4 2.5 psum.23
  197.9 1.4 multiply_convert_fusion.refs_0_
  199.3 44.6 %shard_map.89 = bf16[8,128,1792]{2,1,0:T(8,128)(2,1)S(1)} custom-call(bf16[128,1792]{1,0:T(8,128)(2,1)S(1)} %multiply_convert_fusion.refs_0_), custom_call_target="tpu_custom_call" | custom-call | tf_op jit(solution)/shard_map/pallas_call | solution.py:117
  243.9 4.1 %bitcast_convert_fusion = (bf16[448,1792]{1,0:T(8,128)(2,1)}, f32[1792,448]{0,1:T(8,128)}) fusion(bf16[1024,448]{0,1:T(8,128)(2,1)S(1)} %copy-done.12, bf16[1024,1792]{1,0:T(8,128)(2,1)S(1)} %bitcast.39), kind=kOutput, calls=%fused_computation.3 | convolution fusion | flops 1644969984 | bytes 9404416 | tf_op jit(solution)/shard_map/dot_general | solution.py:343
  248.0 1.1 collective-permute-start
  249.1 3.0 %convert_add_fusion = f32[2,128,1792]{2,1,0:T(8,128)} fusion(bf16[2,128,1792]{2,1,0:T(8,128)(2,1)S(1)} %copy-done.4, f32[2,256,1792]{2,1,0:T(8,128)} %copy-done.7, s32[]{:T(128)S(6)} %select_n.25), kind=kLoop, calls=%fused_computation.4 | loop fusion | flops 917504 | bytes 4587524 | tf_op jit(solution)/shard_map/add | solution.py:329
  252.1 30.6 %collective-permute-done = bf16[448,1792]{1,0:T(8,128)(2,1)} collective-permute-done((bf16[448,1792]{1,0:T(8,128)(2,1)}, bf16[448,1792]{1,0:T(8,128)(2,1)}, u32[]{:S(2)}, u32[]{:S(2)}) %collective-permute-start) | collective-permute-done | bytes 1605664 | tf_op jit(solution)/shard_map/ppermute | solution.py:264
  282.7 3.4 %bitcast_add_fusion = f32[448,1792]{1,0:T(8,128)} fusion(f32[1792,448]{0,1:T(8,128)S(1)} %copy-done.6, bf16[448,1792]{1,0:T(8,128)(2,1)} %collective-permute-done), kind=kLoop, calls=%fused_computation.2 | loop fusion | flops 1605632 | bytes 8028160 | tf_op jit(solution)/shard_map/add | solution.py:265
  (39 shorter events, 1.8 us)
Async XLA Ops:
  7.2 99.0 %copy-start = (bf16[2,256,1792]{2,1,0:T(8,128)(2,1)S(1)}, bf16[2,256,1792]{2,1,0:T(8,128)(2,1)}, u32[]{:S(2)}) copy-start(bf16[2,256,1792]{2,1,0:T(8,128)(2,1)} %param.10) | copy-start | bytes 5505028
  7.2 122.7 %all-reduce.3.cloned.1.call-start = ((), (), s32[]{:S(2)}) async-start(), calls=%async_computation | async-start | bytes 2097152 | tf_op jit(solution)/shard_map/psum | solution.py:295
  11.2 49.0 %copy-start.9 = (s32[128,8]{0,1:T(8,128)S(1)}, s32[128,8]{0,1:T(8,128)}, u32[]{:S(2)}) copy-start(s32[128,8]{0,1:T(8,128)} %param.12) | copy-start | bytes 12292
  11.2 49.0 %copy-start.11 = (s32[128,2]{0,1:T(2,128)S(1)}, s32[128,2]{0,1:T(2,128)}, u32[]{:S(2)}) copy-start(s32[128,2]{0,1:T(2,128)} %param.13) | copy-start | bytes 3076
  11.2 49.0 %copy-start.8 = (f32[1792]{0:T(1024)S(1)}, f32[1792]{0:T(1024)}, u32[]{:S(2)}) copy-start(f32[1792]{0:T(1024)} %param.9) | copy-start | bytes 21508
  106.2 1.8 copy-start.5
  108.0 3.2 %copy-start.10 = (f32[2,256]{1,0:T(2,128)S(1)}, f32[2,256]{1,0:T(2,128)}, u32[]{:S(2)}) copy-start(f32[2,256]{1,0:T(2,128)} %param.11) | copy-start | bytes 6148
  140.4 6.4 %copy-start.1 = (bf16[1024,1792]{1,0:T(8,128)(2,1)S(1)}, bf16[1024,1792]{1,0:T(8,128)(2,1)}, u32[]{:S(2)}) copy-start(bf16[1024,1792]{1,0:T(8,128)(2,1)} %convolution_convert_fusion) | copy-start | bytes 11010052
  145.0 1.8 copy-start.7
  193.4 0.9 copy-start.3
  194.3 0.9 copy-start.2
  199.3 44.6 %copy-start.12 = (bf16[1024,448]{0,1:T(8,128)(2,1)S(1)}, bf16[1024,448]{0,1:T(8,128)(2,1)}, u32[]{:S(2)}) copy-start(bf16[1024,448]{0,1:T(8,128)(2,1)} %param.7) | copy-start | bytes 2752516
  243.9 5.2 %copy-start.4 = (bf16[2,128,1792]{2,1,0:T(8,128)(2,1)S(1)}, bf16[2,128,1792]{2,1,0:T(8,128)(2,1)}, u32[]{:S(2)}) copy-start(bf16[2,128,1792]{2,1,0:T(8,128)(2,1)} %copy-done.3) | copy-start | bytes 2752516
  248.0 34.7 %collective-permute-start = (bf16[448,1792]{1,0:T(8,128)(2,1)}, bf16[448,1792]{1,0:T(8,128)(2,1)}, u32[]{:S(2)}, u32[]{:S(2)}) collective-permute-start(bf16[448,1792]{1,0:T(8,128)(2,1)} %get-tuple-element.30), channel_id=1, source_target_pairs={{0,16},{16,0},{1,17},{17,1},{2,18},{18,2},{3,19},{19,3},{4,20},{20... | collective-permute-start | bytes 4816904 | tf_op jit(solution)/shard_map/ppermute | solution.py:264
  249.1 33.6 %copy-start.6 = (f32[1792,448]{0,1:T(8,128)S(1)}, f32[1792,448]{0,1:T(8,128)}, u32[]{:S(2)}) copy-start(f32[1792,448]{0,1:T(8,128)} %get-tuple-element.31) | copy-start | bytes 9633796
Sparse Core Ops, SparseCore 0:
  111.2 18.6 all-reduce.2

commit v3 on v2

--- a/solution.py
+++ b/solution.py
@@ -44,89 +44,263 @@
     return found
 
 
-def gather_kernel(length, count, *refs):
-    sources, gathered = refs[:count], refs[count : 2 * count]
-    send_sem, recv_sem = refs[2 * count :]
+def hop_copy(held, block, cols, way, part, sems, device):
+    send_sem, recv_sem = sems
+    return pltpu.make_async_remote_copy(
+        src_ref=held.at[block, :, cols],
+        dst_ref=held.at[block, :, cols],
+        send_sem=send_sem.at[part, way, block],
+        recv_sem=recv_sem.at[part, block],
+        device_id=device,
+        device_id_type=MESH,
+    )
+
+
+def devices_of(z, low):
+    return (
+        at("label", z * FAST + 1 - low),
+        at("label", (z + 1) * FAST + low),
+        at("label", (z - 1) * FAST + low),
+    )
+
+
+def send_own(z, low, length, held, cols, part, sems):
+    own = z * FAST + low
+    across, up, down = devices_of(z, low)
+    if z + 1 < length:
+        hop_copy(held, own, cols, 1, part, sems, up).start()
+    if z > 0:
+        hop_copy(held, own, cols, 2, part, sems, down).start()
+    hop_copy(held, own, cols, 0, part, sems, across).start()
+
+
+def forward(z, low, length, held, cols, part, sems):
+    across, up, down = devices_of(z, low)
+    for step in range(1, length):
+        if z - step >= 0:
+            block = (z - step) * FAST + low
+            hop_copy(held, block, cols, 0, part, sems, across).wait_recv()
+            if z + 1 < length:
+                hop_copy(held, block, cols, 1, part, sems, up).start()
+            hop_copy(held, block, cols, 0, part, sems, across).start()
+        if z + step < length:
+            block = (z + step) * FAST + low
+            hop_copy(held, block, cols, 0, part, sems, across).wait_recv()
+            if z > 0:
+                hop_copy(held, block, cols, 2, part, sems, down).start()
+            hop_copy(held, block, cols, 0, part, sems, across).start()
+
+
+def wait_sent(z, low, length, held, cols, part, sems):
+    across, up, down = devices_of(z, low)
+    for t in range(length):
+        block = t * FAST + low
+        hop_copy(held, block, cols, 0, part, sems, across).wait_send()
+        if t <= z and z + 1 < length:
+            hop_copy(held, block, cols, 1, part, sems, up).wait_send()
+        if t >= z and z > 0:
+            hop_copy(held, block, cols, 2, part, sems, down).wait_send()
+
+
+def by_place(length, high, body):
+    for z in range(length):
+        pl.when(high == z)(functools.partial(body, z))
+
+
+def score_kernel(length, rows_ref, target_ref, head_ref, held, targets, scores, *rest):
+    leaving, coming, send_sem, recv_sem, pair_send, pair_recv = rest
     high, low = spot()
-
-    def copies(way, block, first, device):
-        return [
-            pltpu.make_async_remote_copy(
-                src_ref=sources[i] if first else gathered[i].at[block],
-                dst_ref=gathered[i].at[block],
-                send_sem=send_sem.at[i, way, block],
-                recv_sem=recv_sem.at[i, block],
-                device_id=device,
-                device_id_type=MESH,
-            )
-            for i in range(count)
-        ]
-
-    def branch(z):
-        across = at("label", z * FAST + 1 - low)
-        up = at("label", (z + 1) * FAST + low)
-        down = at("label", (z - 1) * FAST + low)
-        greet(neighbours(high, low, z, length))
-        sent = []
-
-        def send(way, block, first, device):
-            made = copies(way, block, first, device)
-            for copy in made:
-                copy.start()
-            sent.extend(made)
-
-        def arrived(block):
-            for copy in copies(0, block, False, across):
-                copy.wait_recv()
-
-        own = z * FAST + low
-        if z + 1 < length:
-            send(1, own, True, up)
-        if z > 0:
-            send(2, own, True, down)
-        send(0, own, True, across)
-        for i in range(count):
-            gathered[i][own] = sources[i][...]
-        for step in range(1, length):
-            if z - step >= 0:
-                block = (z - step) * FAST + low
-                arrived(block)
-                if z + 1 < length:
-                    send(1, block, False, up)
-                send(0, block, False, across)
-            if z + step < length:
-                block = (z + step) * FAST + low
-                arrived(block)
-                if z > 0:
-                    send(2, block, False, down)
-                send(0, block, False, across)
-        for other in sorted(range(length), key=lambda t: abs(t - z)):
-            arrived(other * FAST + 1 - low)
-        for copy in sent:
-            copy.wait_send()
-
-    for z in range(length):
-        pl.when(high == z)(functools.partial(branch, z))
-
-
-def gather_label(arrays, number):
+    own = high * FAST + low
+    every = slice(None)
+    sems = (send_sem, recv_sem)
+    sibling = at("tensor", 1 - lax.axis_index("tensor"))
+    held[own] = rows_ref[...]
+    targets[own] = target_ref[...]
+
+    def start(z):
+        greet(neighbours(high, low, z, length) + [sibling])
+        send_own(z, low, length, targets, every, 1, sems)
+        send_own(z, low, length, held, every, 0, sems)
+        forward(z, low, length, targets, every, 1, sems)
+        forward(z, low, length, held, every, 0, sems)
+
+    by_place(length, high, start)
+
+    def pair(block):
+        return pltpu.make_async_remote_copy(
+            src_ref=leaving.at[block],
+            dst_ref=coming.at[block],
+            send_sem=pair_send.at[block],
+            recv_sem=pair_recv.at[block],
+            device_id=sibling,
+            device_id_type=MESH,
+        )
+
+    def score(block):
+        part = lax.dot_general(
+            held[block], head_ref[...], (((1,), (1,)), ((), ())), preferred_element_type=F32
+        )
+        scores[block] = part
+        leaving[block] = part.astype(BF16)
+        pair(block).start()
+
+    half = high // (length // 2)
+
+    def visit(i, carry):
+        side = i // length
+        step = lax.rem(i, length)
+        t = step + half * (length - 1 - 2 * step)
+        block = t * FAST + low + side * (1 - 2 * low)
+        across = at("label", high * FAST + 1 - low)
+
+        @pl.when(side == 1)
+        def _():
+            hop_copy(targets, block, every, 0, 1, sems, across).wait_recv()
+            hop_copy(held, block, every, 0, 0, sems, across).wait_recv()
+
+        score(block)
+        return carry
+
+    lax.fori_loop(0, FAST * length, visit, 0)
+
+    def finish(i, carry):
+        side = i // length
+        step = lax.rem(i, length)
+        t = step + half * (length - 1 - 2 * step)
+        block = t * FAST + low + side * (1 - 2 * low)
+        pair(block).wait()
+        scores[block] = scores[block] + coming[block].astype(F32)
+        return carry
+
+    lax.fori_loop(0, FAST * length, finish, 0)
+
+    def last(z):
+        wait_sent(z, low, length, targets, every, 1, sems)
+        wait_sent(z, low, length, held, every, 0, sems)
+
+    by_place(length, high, last)
+
+
+def gather_score(rows, targets, head, number):
     devices = lax.axis_size("label")
-    if devices != 4 * FAST:
-        return [lax.all_gather(a, "label", axis=0) for a in arrays]
-    count = len(arrays)
+    here, width = rows.shape
+    labels = head.shape[0]
+    if devices != 4 * FAST or lax.axis_size("tensor") != 2:
+        rows = lax.all_gather(rows, "label", axis=0)
+        targets = lax.all_gather(targets, "label", axis=0)
+        part = jnp.einsum("nrd,jd->nrj", rows, head, preferred_element_type=F32)
+        return rows, targets, lax.psum(part.astype(BF16), "tensor").astype(F32)
     return pl.pallas_call(
-        functools.partial(gather_kernel, devices // FAST, count),
-        out_shape=[jax.ShapeDtypeStruct((devices,) + a.shape, a.dtype) for a in arrays],
-        in_specs=[pl.BlockSpec(memory_space=pltpu.VMEM)] * count,
-        out_specs=[pl.BlockSpec(memory_space=pltpu.VMEM)] * count,
-        scratch_shapes=[
-            pltpu.SemaphoreType.DMA((count, 3, devices)),
-            pltpu.SemaphoreType.DMA((count, devices)),
+        functools.partial(score_kernel, devices // FAST),
+        out_shape=[
+            jax.ShapeDtypeStruct((devices, here, width), rows.dtype),
+            jax.ShapeDtypeStruct((devices,) + targets.shape, targets.dtype),
+            jax.ShapeDtypeStruct((devices, here, labels), F32),
+        ],
+        in_specs=[pl.BlockSpec(memory_space=pltpu.VMEM)] * 3,
+        out_specs=[pl.BlockSpec(memory_space=pltpu.VMEM)] * 3,
+        scratch_shapes=[pltpu.VMEM((devices, here, labels), BF16)] * 2
+        + [
+            pltpu.SemaphoreType.DMA((2, 3, devices)),
+            pltpu.SemaphoreType.DMA((2, devices)),
+            pltpu.SemaphoreType.DMA((devices,)),
+            pltpu.SemaphoreType.DMA((devices,)),
         ],
         compiler_params=pltpu.CompilerParams(
             collective_id=number, has_side_effects=True, vmem_limit_bytes=VMEM_LIMIT
         ),
-    )(*arrays)
+    )(rows, targets, head)
+
+
+def weight_kernel(length, cuts, grad_ref, turned_ref, part_ref, other, held, leaving, *rest):
+    send_sem, recv_sem, pair_send, pair_recv = rest
+    high, low = spot()
+    own = high * FAST + low
+    sems = (send_sem, recv_sem)
+    beside = at("dp", 1 - lax.axis_index("dp"))
+    across = at("label", high * FAST + 1 - low)
+    held[own] = grad_ref[...]
+
+    def start(z):
+        greet(neighbours(high, low, z, length) + [beside])
+        send_own(z, low, length, held, cuts[0], 0, sems)
+
+    def onward(part, z):
+        forward(z, low, length, held, cuts[part], part, sems)
+        if part + 1 < len(cuts):
+            send_own(z, low, length, held, cuts[part + 1], part + 1, sems)
+
+    def exchange(part):
+        return pltpu.make_async_remote_copy(
+            src_ref=leaving.at[:, cuts[part]],
+            dst_ref=other.at[:, cuts[part]],
+            send_sem=pair_send.at[part],
+            recv_sem=pair_recv.at[part],
+            device_id=beside,
+            device_id_type=MESH,
+        )
+
+    by_place(length, high, start)
+    for part, cols in enumerate(cuts):
+        by_place(length, high, functools.partial(onward, part))
+        for t in range(length):
+            block = t * FAST + 1 - low
+            hop_copy(held, block, cols, 0, part, sems, across).wait_recv()
+        grads = held[:, :, cols]
+        product = jnp.dot(
+            turned_ref[...],
+            grads.reshape(grads.shape[0] * grads.shape[1], grads.shape[2]),
+            preferred_element_type=F32,
+        )
+        part_ref[:, cols] = product
+        leaving[:, cols] = product.astype(BF16)
+        exchange(part).start()
+    for part in range(len(cuts)):
+        exchange(part).wait()
+
+    def last(z):
+        for part, cols in enumerate(cuts):
+            wait_sent(z, low, length, held, cols, part, sems)
+
+    by_place(length, high, last)
+
+
+def weight_grad(hidden, grad, number):
+    devices = lax.axis_size("label")
+    here, width = grad.shape
+    features = hidden.shape[1]
+    if devices != 4 * FAST or lax.axis_size("dp") != 2:
+        grads = lax.all_gather(grad, "label", axis=0, tiled=True)
+        return sum_over_dp(
+            lax.dot_general(
+                hidden, grads, (((0,), (0,)), ((), ())), preferred_element_type=F32
+            )
+        )
+    tiles = width // 128
+    pieces = min(4, tiles)
+    edges = [-(-tiles * i // pieces) * 128 for i in range(pieces)] + [width]
+    cuts = [slice(edges[i], edges[i + 1]) for i in range(pieces)]
+    part, other = pl.pallas_call(
+        functools.partial(weight_kernel, devices // FAST, cuts),
+        out_shape=[
+            jax.ShapeDtypeStruct((features, width), F32),
+            jax.ShapeDtypeStruct((features, width), BF16),
+        ],
+        in_specs=[pl.BlockSpec(memory_space=pltpu.VMEM)] * 2,
+        out_specs=[pl.BlockSpec(memory_space=pltpu.VMEM)] * 2,
+        scratch_shapes=[
+            pltpu.VMEM((devices, here, width), BF16),
+            pltpu.VMEM((features, width), BF16),
+            pltpu.SemaphoreType.DMA((pieces, 3, devices)),
+            pltpu.SemaphoreType.DMA((pieces, devices)),
+            pltpu.SemaphoreType.DMA((pieces,)),
+            pltpu.SemaphoreType.DMA((pieces,)),
+        ],
+        compiler_params=pltpu.CompilerParams(
+            collective_id=number, has_side_effects=True, vmem_limit_bytes=VMEM_LIMIT
+        ),
+    )(grad, hidden.T)
+    return part + other.astype(F32)
 
 
 def scatter_kernel(length, swap, *refs):
@@ -284,15 +458,11 @@
     squares = lax.psum(jnp.sum(pooled * pooled, axis=1), "tensor")
     inverse = lax.rsqrt(squares / full_width + EPSILON)
     embedded = (pooled * inverse[:, None] * enc_gain[None, :]).astype(BF16)
-    rows, targets = gather_label([embedded, targets], 1)
+    rows, targets, scores = gather_score(embedded, targets, head, 1)
+    scores = scores.reshape(labels_n * rows_here, -1)
     rows = rows.reshape(labels_n * rows_here, width_half)
     targets = jnp.swapaxes(targets, 1, 2).reshape(labels_n * rows_here, -1)
     all_blocks, all_offsets = targets[:, :slots], targets[:, slots : slots + pos_count]
-
-    partial = lax.dot_general(
-        rows, head, (((1,), (1,)), ((), ())), preferred_element_type=F32
-    )
-    scores = lax.psum(partial.astype(BF16), "tensor").astype(F32)
 
     label_ids = jnp.arange(block_size, dtype=jnp.int32)[None, :]
     first = lax.axis_index("label") * blocks_dev
@@ -338,12 +508,7 @@
     pooled_grad = (
         inverse[:, None] * (scaled - pooled * (inverse * inverse * row_dot / full_width)[:, None])
     ).astype(BF16)
-    (all_grad,) = gather_label([pooled_grad], 3)
-    all_grad = all_grad.reshape(labels_n * rows_here, width_half)
-    weight_part = lax.dot_general(
-        hidden, all_grad, (((0,), (0,)), ((), ())), preferred_element_type=F32
-    )
-    enc_grad = sum_over_dp(weight_part)
+    enc_grad = weight_grad(hidden, pooled_grad, 3)
     return (enc_grad, head_grad)
 
 

time: 293 us -> 233 us (0.80)
  waiting for transfers between devices: 49.3 us -> 0 us
  Pallas kernels: 183 us -> 201 us
  between operations: 14.3 us -> 0.8 us
  matrix products: 19.5 us -> 9.92 us
  other arithmetic: 12.7 us -> 8.53 us
    ppermute x1 -> x0, waiting for transfers between devices: 30.6 us -> none  [sum_over_dp(): other = lax.ppermute(part.astype(BF16), 'dp', [(0, 1), (1, 0)])]
    psum x1 -> x0, waiting for transfers between devices: 18.6 us -> none  [shards(): scores = lax.psum(partial.astype(BF16), 'tensor').astype(F32)]
    pallas_call x2, Pallas kernels: 90.3 us -> 109 us  [the longest x1 60.3 us: weight_grad(): pl.pallas_call(functools.partial(weight_kernel, devices // FAST, cuts), o...]
    dot_general x2 -> x0, matrix products: 7.13 us -> none  [the longest x1 4.07 us: shards(): lax.dot_general(hidden, all_grad, (((0,), (0,)), ((), ())), preferred_ele...]
  transfers between devices with their start and end apart: 2 -> 0, of which waited for: 2 -> 0; matrix products, arithmetic and copies ran while one was open for 1% -> 0% of each run, Pallas kernels for 0% -> 0%
where the time goes in v3:
time: 233 us
  Pallas kernels  201 us (86%)
  matrix products  9.92 us (4%)
  other arithmetic  8.53 us (4%)
  local copies, waits for them, and re-layouts  7.5 us (3%)
  blocking collectives  4.92 us (2%)
    pallas_call x2, Pallas kernels, scatter_label(): pl.pallas_call(functools.partial(scatter_kernel, length, swap), out_shape...  92.2 us
    pallas_call x1, Pallas kernels, weight_grad(): pl.pallas_call(functools.partial(weight_kernel, devices // FAST, cuts), o...  60.3 us
    pallas_call x1, Pallas kernels, gather_score(): pl.pallas_call(functools.partial(score_kernel, devices // FAST), out_shap...  48.4 us
    unnamed x16, local copies, waits for them, and re-layouts  5.06 us

profile of v3, /device:TPU:0, one launch (start us, length us, event | category | flops | bytes accessed | tf_op | source)
XLA Modules:
  0.0 232.6 jit_solution(10117199981129306227)
XLA Ops:
  0.7 0.8 broadcast_multiply_fusion.1
  1.5 0.7 add_bitcast_fusion
  2.2 3.3 %convolution_convert_fusion.1 = bf16[1024,1792]{1,0:T(8,128)(2,1)S(1)} fusion(bf16[1024,448]{0,1:T(8,128)(2,1)} %param.7, bf16[448,1792]{1,0:T(8,128)(2,1)S(1)} %copy-done), kind=kOutput, calls=%fused_computation.1 | convolution fusion | flops 1646002176 | bytes 6193152 | tf_op jit(solution)/shard_map/dot_general | solution.py:456
  5.5 46.4 %shard_map.86 = f32[128,1792]{1,0:T(8,128)S(1)} custom-call(bf16[8,128,1792]{2,1,0:T(8,128)(2,1)S(1)} %bitcast.31), custom_call_target="tpu_custom_call" | custom-call | tf_op jit(solution)/shard_map/pallas_call | solution.py:417
  51.9 0.1 multiply_reduce_fusion.1
  52.0 2.5 %psum.14 = f32[128]{0:T(128)S(1)} all-reduce(f32[128]{0:T(128)S(1)} %multiply_reduce_fusion.1), channel_id=1, replica_groups=mesh['dp'=2,'label'=8,'tensor'=2] {'tensor'}, use_global_device_ids=true, to_apply=%region_1.2 | all-reduce | flops 128 | bytes 1024 | tf_op jit(solution)/shard_map/psum | solution.py:458
  54.5 0.1 multiply_convert_fusion.1.rows_ref
  54.7 1.5 copy-done.1
  56.2 48.4 %shard_map.87 = (bf16[8,128,1792]{2,1,0:T(8,128)(2,1)S(1)}, s32[8,16,128]{2,1,0:T(8,128)S(1)}, f32[8,128,512]{2,1,0:T(8,128)S(1)}) custom-call(bf16[128,1792]{1,0:T(8,128)(2,1)S(1)} %multiply_convert_fusion.1.rows_ref, s32[16,128]{1,0:T(8,128)S(1)} %pad.4.target_ref, bf16[512,1792]{1,0:T(8,128)(2,1)S(1)} %bitcast.33), custom_call_target="tpu_custom_call" | custom-call | tf_op jit(solution)/shard_map/pallas_call | solution.py:193
  104.6 1.8 copy-done.4
  106.5 1.8 select_convert_fusion.1
  108.4 0.8 copy-done.5
  109.2 1.1 fusion.6
  110.2 2.3 copy.11
  112.5 4.6 %fusion.11 = f32[2,256,1792]{2,1,0:T(8,128)S(1)} fusion(bf16[2,256,1024]{2,1,0:T(8,128)(2,1)} %bitcast.37, bf16[1024,1792,1]{1,0,2:T(8,128)(2,1)} %bitcast.36), kind=kOutput, calls=%fused_computation.41 | convolution fusion | flops 1879048192 | bytes 8388608 | tf_op jit(solution)/shard_map/dot_general | solution.py:490
  117.2 2.1 convolution_convert_fusion
  119.3 45.8 %shard_map.88 = (f32[128,1792]{1,0:T(8,128)S(1)}, bf16[2,128,1792]{2,1,0:T(8,128)(2,1)S(1)}) custom-call(bf16[8,128,1792]{2,1,0:T(8,128)(2,1)S(1)} %bitcast.30, bf16[2,128,1792]{2,1,0:T(8,128)(2,1)S(1)} %dynamic-slice_convert_fusion.refs_1_), custom_call_target="tpu_custom_call" | custom-call | tf_op jit(solution)/shard_map/pallas_call | solution.py:417
  165.1 1.4 convert_add_fusion.1
  166.5 0.2 multiply_reduce_fusion
  166.6 2.5 %psum.15 = f32[128]{0:T(128)S(1)} all-reduce(f32[128]{0:T(128)S(1)} %multiply_reduce_fusion), channel_id=1, replica_groups=mesh['dp'=2,'label'=8,'tensor'=2] {'tensor'}, use_global_device_ids=true, to_apply=%region_5.6 | all-reduce | flops 128 | bytes 1024 | tf_op jit(solution)/shard_map/psum | solution.py:507
  169.1 0.2 multiply_convert_fusion.grad_ref
  169.3 0.9 copy-done.3
  170.3 60.3 %shard_map.89 = (f32[448,1792]{1,0:T(8,128)S(1)}, bf16[448,1792]{1,0:T(8,128)(2,1)S(1)}) custom-call(bf16[128,1792]{1,0:T(8,128)(2,1)S(1)} %multiply_convert_fusion.grad_ref, bf16[448,1024]{1,0:T(8,128)(2,1)S(1)} %bitcast.35), custom_call_target="tpu_custom_call" | custom-call | tf_op jit(solution)/shard_map/pallas_call | solution.py:283
  230.6 2.0 convert_add_fusion
  (21 shorter events, 0.3 us)
Async XLA Ops:
  0.6 1.6 copy-start
  5.5 49.0 %copy-start.7 = (f32[1792]{0:T(1024)S(1)}, f32[1792]{0:T(1024)}, u32[]{:S(2)}) copy-start(f32[1792]{0:T(1024)} %param.9) | copy-start | bytes 21508
  54.7 1.5 copy-start.1
  104.6 1.8 copy-start.4
  108.4 0.8 copy-start.5
  112.5 4.7 %copy-start.2 = (bf16[2,256,1792]{2,1,0:T(8,128)(2,1)S(1)}, bf16[2,256,1792]{2,1,0:T(8,128)(2,1)}, u32[]{:S(2)}) copy-start(bf16[2,256,1792]{2,1,0:T(8,128)(2,1)} %param.10) | copy-start | bytes 5505028
  112.5 4.7 %copy-start.6 = (bf16[1024,256]{1,0:T(8,128)(2,1)S(1)}, bf16[1024,256]{1,0:T(8,128)(2,1)}, u32[]{:S(2)}) copy-start(bf16[1024,256]{1,0:T(8,128)(2,1)} %copy-done.5) | copy-start | bytes 1572868
  169.1 1.2 copy-start.3

commit v4 on v3

--- a/solution.py
+++ b/solution.py
@@ -226,9 +226,9 @@
         send_own(z, low, length, held, cuts[0], 0, sems)
 
     def onward(part, z):
+        if part > 0:
+            send_own(z, low, length, held, cuts[part], part, sems)
         forward(z, low, length, held, cuts[part], part, sems)
-        if part + 1 < len(cuts):
-            send_own(z, low, length, held, cuts[part + 1], part + 1, sems)
 
     def exchange(part):
         return pltpu.make_async_remote_copy(
@@ -241,8 +241,10 @@
         )
 
     by_place(length, high, start)
+    by_place(length, high, functools.partial(onward, 0))
     for part, cols in enumerate(cuts):
-        by_place(length, high, functools.partial(onward, part))
+        if part + 1 < len(cuts):
+            by_place(length, high, functools.partial(onward, part + 1))
         for t in range(length):
             block = t * FAST + 1 - low
             hop_copy(held, block, cols, 0, part, sems, across).wait_recv()
@@ -305,8 +307,8 @@
 
 def scatter_kernel(length, swap, *refs):
     if swap:
-        parts, theirs, out, other = refs[:4]
-        rest = refs[4:]
+        parts, slopes, rows_ref, out, mine, other, theirs = refs[:7]
+        rest = refs[7:]
     else:
         parts, out = refs[:2]
         rest = refs[2:]
@@ -325,31 +327,65 @@
             device_id_type=MESH,
         )
 
+    if swap:
+        me = lax.axis_index("dp")
+        exchange = pltpu.make_async_remote_copy(
+            src_ref=theirs,
+            dst_ref=other,
+            send_sem=swap_sem.at[0],
+            recv_sem=swap_sem.at[1],
+            device_id=at("dp", 1 - me),
+            device_id_type=MESH,
+        )
+
+    def order_of(z):
+        return sorted(range(length), key=lambda t: (-abs(t - z), -t))
+
+    def crossing(z, t):
+        across = at("label", z * FAST + 1 - low)
+        return remote(parts.at[t * FAST + 1 - low], crossed.at[t], 0, t, across)
+
+    def begin(z):
+        greeted = neighbours(high, low, z, length)
+        if swap:
+            greeted.append(at("dp", 1 - me))
+        greet(greeted)
+        for t in order_of(z)[:2]:
+            crossing(z, t).start()
+
+    def head_products():
+        count, half = theirs.shape[:2]
+
+        def product(n, side):
+            span = pl.ds(pl.multiple_of((n * 2 + side) * half, half), half)
+            return lax.dot_general(
+                slopes[:, span],
+                rows_ref[...],
+                (((0,), (0,)), ((), ())),
+                preferred_element_type=F32,
+            )
+
+        def for_other(n, carry):
+            theirs[n] = product(n, 1 - me).astype(BF16)
+            return carry
+
+        def for_own(n, carry):
+            mine[n] = product(n, me)
+            return carry
+
+        lax.fori_loop(0, count, for_other, 0)
+        exchange.start()
+        lax.fori_loop(0, count, for_own, 0)
+
     def branch(z):
         across = at("label", z * FAST + 1 - low)
         up = at("label", (z + 1) * FAST + low)
         down = at("label", (z - 1) * FAST + low)
-        greeted = neighbours(high, low, z, length)
-        if swap:
-            beside = at("dp", 1 - lax.axis_index("dp"))
-            greeted.append(beside)
-        greet(greeted)
-        sent = []
-        if swap:
-            exchange = pltpu.make_async_remote_copy(
-                src_ref=theirs,
-                dst_ref=other,
-                send_sem=swap_sem.at[0],
-                recv_sem=swap_sem.at[1],
-                device_id=beside,
-                device_id_type=MESH,
-            )
-            exchange.start()
-
-        order = sorted(range(length), key=lambda t: (-abs(t - z), -t))
+        order = order_of(z)
+        sent = [crossing(z, t) for t in order[:2]]
 
         def cross(t):
-            copy = remote(parts.at[t * FAST + 1 - low], crossed.at[t], 0, t, across)
+            copy = crossing(z, t)
             copy.start()
             sent.append(copy)
 
@@ -367,8 +403,6 @@
 
             lax.fori_loop(0, rows // tile, body, 0)
 
-        for t in order[:2]:
-            cross(t)
         for place, t in enumerate(order):
             remote(parts.at[0], crossed.at[t], 0, t, across).wait_recv()
             if place + 2 < length:
@@ -393,33 +427,43 @@
             sent.append(copy)
         for copy in sent:
             copy.wait_send()
-        if swap:
-            exchange.wait()
-
-    for z in range(length):
-        pl.when(high == z)(functools.partial(branch, z))
-
-
-def scatter_label(parts, number, theirs=None):
-    devices, rows, width = parts.shape
-    swap = theirs is not None
-    if devices != 4 * FAST:
+
+    by_place(length, high, begin)
+    if swap:
+        head_products()
+    by_place(length, high, branch)
+    if swap:
+        exchange.wait()
+
+
+def scatter_label(parts, number, slopes=None, rows=None, count=0):
+    devices, here, width = parts.shape
+    swap = slopes is not None
+    if devices != 4 * FAST or (swap and lax.axis_size("dp") != 2):
         out = lax.psum_scatter(parts, "label", scatter_dimension=0, tiled=False).astype(F32)
-        if swap:
-            return out, lax.ppermute(theirs, "dp", [(0, 1), (1, 0)])
-        return out
+        if not swap:
+            return out
+        whole = lax.dot_general(
+            slopes, rows, (((0,), (0,)), ((), ())), preferred_element_type=F32
+        ).reshape(count, -1, width)
+        whole = lax.psum_scatter(whole.astype(BF16), "dp", scatter_dimension=1, tiled=True)
+        return out, whole.astype(F32)
     length = devices // FAST
-    out_shape = [jax.ShapeDtypeStruct((rows, width), F32)]
+    out_shape = [jax.ShapeDtypeStruct((here, width), F32)]
     operands = [parts]
+    scratch = []
     if swap:
-        out_shape.append(jax.ShapeDtypeStruct(theirs.shape, theirs.dtype))
-        operands.append(theirs)
+        share = (count, slopes.shape[1] // count // 2, width)
+        out_shape += [jax.ShapeDtypeStruct(share, F32), jax.ShapeDtypeStruct(share, BF16)]
+        operands += [slopes, rows]
+        scratch = [pltpu.VMEM(share, BF16)]
     outs = pl.pallas_call(
         functools.partial(scatter_kernel, length, swap),
         out_shape=out_shape,
         in_specs=[pl.BlockSpec(memory_space=pltpu.VMEM)] * len(operands),
-        out_specs=[pl.BlockSpec(memory_space=pltpu.VMEM)] * len(operands),
-        scratch_shapes=[pltpu.VMEM((length, rows, width), BF16)] * 5
+        out_specs=[pl.BlockSpec(memory_space=pltpu.VMEM)] * len(out_shape),
+        scratch_shapes=scratch
+        + [pltpu.VMEM((length, here, width), BF16)] * 5
         + [
             pltpu.SemaphoreType.DMA((3, length)),
             pltpu.SemaphoreType.DMA((3, length)),
@@ -429,7 +473,9 @@
             collective_id=number, has_side_effects=True, vmem_limit_bytes=VMEM_LIMIT
         ),
     )(*operands)
-    return outs if swap else outs[0]
+    if not swap:
+        return outs[0]
+    return outs[0], outs[1] + outs[2].astype(F32)
 
 
 def sum_over_dp(part):
@@ -487,21 +533,7 @@
 
     back = jnp.dot(slopes, head, preferred_element_type=F32).astype(BF16)
     back = back.reshape(labels_n, rows_here, width_half)
-    head_partial = lax.dot_general(
-        slopes, rows, (((0,), (0,)), ((), ())), preferred_element_type=F32
-    ).reshape(blocks_dev, block_size, width_half)
-    if lax.axis_size("dp") == 2:
-        half = block_size // 2
-        me = lax.axis_index("dp")
-        mine = lax.dynamic_slice_in_dim(head_partial, me * half, half, 1)
-        theirs = lax.dynamic_slice_in_dim(head_partial, (1 - me) * half, half, 1)
-        embed_grad, other = scatter_label(back, 2, theirs.astype(BF16))
-        head_grad = mine + other.astype(F32)
-    else:
-        embed_grad = scatter_label(back, 2)
-        head_grad = lax.psum_scatter(
-            head_partial.astype(BF16), "dp", scatter_dimension=1, tiled=True
-        ).astype(F32)
+    embed_grad, head_grad = scatter_label(back, 2, slopes, rows, blocks_dev)
 
     scaled = embed_grad * enc_gain[None, :]
     row_dot = lax.psum(jnp.sum(scaled * pooled, axis=1), "tensor")

time: 233 us -> 227 us (0.974)
  Pallas kernels: 201 us -> 206 us
  local copies, waits for them, and re-layouts: 7.5 us -> 2.54 us
  matrix products: 9.92 us -> 5.36 us
    pallas_call x1, Pallas kernels: 60.3 us -> 65.2 us  [weight_grad(): pl.pallas_call(functools.partial(weight_kernel, devices // FAST, cuts), o...]
    dot_general x1 -> x0, matrix products: 4.56 us -> none  [shards(): lax.dot_general(slopes, rows, (((0,), (0,)), ((), ())), preferred_element...]
    unnamed x16 -> x8, local copies, waits for them, and re-layouts: 5.06 us -> 2.46 us
where the time goes in v4:
time: 227 us
  Pallas kernels  206 us (91%)
  other arithmetic  7.55 us (3%)
  matrix products  5.36 us (2%)
  blocking collectives  4.92 us (2%)
  local copies, waits for them, and re-layouts  2.54 us (1%)
    pallas_call x2, Pallas kernels, scatter_label(): pl.pallas_call(functools.partial(scatter_kernel, length, swap), out_shape...  92.2 us
    pallas_call x1, Pallas kernels, weight_grad(): pl.pallas_call(functools.partial(weight_kernel, devices // FAST, cuts), o...  65.2 us
    pallas_call x1, Pallas kernels, gather_score(): pl.pallas_call(functools.partial(score_kernel, devices // FAST), out_shap...  48.5 us

profile of v4, /device:TPU:0, one launch (start us, length us, event | category | flops | bytes accessed | tf_op | source)
XLA Modules:
  0.0 226.9 jit_solution(12984086360443559644)
XLA Ops:
  0.6 0.0 copy-start
  0.7 0.8 broadcast_multiply_fusion.1
  1.5 0.7 add_bitcast_fusion
  2.2 3.3 %convolution_convert_fusion.1 = bf16[1024,1792]{1,0:T(8,128)(2,1)S(1)} fusion(bf16[1024,448]{0,1:T(8,128)(2,1)} %param.7, bf16[448,1792]{1,0:T(8,128)(2,1)S(1)} %copy-done), kind=kOutput, calls=%fused_computation.1 | convolution fusion | flops 1646002176 | bytes 6193152 | tf_op jit(solution)/shard_map/dot_general | solution.py:502
  5.5 0.0 copy-start.3
  5.5 46.4 %shard_map.86 = f32[128,1792]{1,0:T(8,128)S(1)} custom-call(bf16[8,128,1792]{2,1,0:T(8,128)(2,1)S(1)} %bitcast.25), custom_call_target="tpu_custom_call" | custom-call | tf_op jit(solution)/shard_map/pallas_call | solution.py:460
  51.9 0.1 multiply_reduce_fusion.1
  52.0 2.5 %psum.14 = f32[128]{0:T(128)S(1)} all-reduce(f32[128]{0:T(128)S(1)} %multiply_reduce_fusion.1), channel_id=1, replica_groups=mesh['dp'=2,'label'=8,'tensor'=2] {'tensor'}, use_global_device_ids=true, to_apply=%region_1.2 | all-reduce | flops 128 | bytes 1024 | tf_op jit(solution)/shard_map/psum | solution.py:504
  54.5 0.1 multiply_convert_fusion.1.rows_ref
  54.7 0.0 copy-start.1
  54.7 1.5 copy-done.1
  56.2 48.5 %shard_map.87 = (bf16[8,128,1792]{2,1,0:T(8,128)(2,1)S(1)}, s32[8,16,128]{2,1,0:T(8,128)S(1)}, f32[8,128,512]{2,1,0:T(8,128)S(1)}) custom-call(bf16[128,1792]{1,0:T(8,128)(2,1)S(1)} %multiply_convert_fusion.1.rows_ref, s32[16,128]{1,0:T(8,128)S(1)} %pad.4.target_ref, bf16[512,1792]{1,0:T(8,128)(2,1)S(1)} %bitcast.27), custom_call_target="tpu_custom_call" | custom-call | tf_op jit(solution)/shard_map/pallas_call | solution.py:193
  104.7 0.1 slice_reduce_fusion.1
  104.8 1.8 select_convert_fusion.1
  106.6 0.1 pad_maximum_fusion.refs_1_
  106.7 2.1 convolution_convert_fusion
  108.8 45.8 %shard_map.88 = (f32[128,1792]{1,0:T(8,128)S(1)}, f32[2,128,1792]{2,1,0:T(8,128)S(1)}, bf16[2,128,1792]{2,1,0:T(8,128)(2,1)S(1)}) custom-call(bf16[8,128,1792]{2,1,0:T(8,128)(2,1)S(1)} %bitcast.24, bf16[1024,512]{1,0:T(8,128)(2,1)S(1)} %pad_maximum_fusion.refs_1_, bf16[1024,1792]{1,0:T(8,128)(2,1)S(1)} %bitcast.23), custom_call_target="tpu_custom_call" | custom-call | tf_op jit(solution)/shard_map/pallas_call | solution.py:460
  154.6 1.4 convert_add_fusion.1
  155.9 0.2 multiply_reduce_fusion
  156.1 2.5 %psum.15 = f32[128]{0:T(128)S(1)} all-reduce(f32[128]{0:T(128)S(1)} %multiply_reduce_fusion), channel_id=1, replica_groups=mesh['dp'=2,'label'=8,'tensor'=2] {'tensor'}, use_global_device_ids=true, to_apply=%region_5.6 | all-reduce | flops 128 | bytes 1024 | tf_op jit(solution)/shard_map/psum | solution.py:539
  158.6 0.2 multiply_convert_fusion.grad_ref
  158.8 0.9 copy-done.2
  159.8 65.2 %shard_map.89 = (f32[448,1792]{1,0:T(8,128)S(1)}, bf16[448,1792]{1,0:T(8,128)(2,1)S(1)}) custom-call(bf16[128,1792]{1,0:T(8,128)(2,1)S(1)} %multiply_convert_fusion.grad_ref, bf16[448,1024]{1,0:T(8,128)(2,1)S(1)} %bitcast.29), custom_call_target="tpu_custom_call" | custom-call | tf_op jit(solution)/shard_map/pallas_call | solution.py:285
  224.9 2.0 convert_add_fusion
  (10 shorter events, 0.1 us)
Async XLA Ops:
  0.6 1.6 copy-start
  5.5 49.0 %copy-start.3 = (f32[1792]{0:T(1024)S(1)}, f32[1792]{0:T(1024)}, u32[]{:S(2)}) copy-start(f32[1792]{0:T(1024)} %param.9) | copy-start | bytes 21508
  54.7 1.5 copy-start.1
  158.6 1.2 copy-start.2

commit v5 on v4

--- a/solution.py
+++ b/solution.py
@@ -121,8 +121,8 @@
         greet(neighbours(high, low, z, length) + [sibling])
         send_own(z, low, length, targets, every, 1, sems)
         send_own(z, low, length, held, every, 0, sems)
+        forward(z, low, length, held, every, 0, sems)
         forward(z, low, length, targets, every, 1, sems)
-        forward(z, low, length, held, every, 0, sems)
 
     by_place(length, high, start)
 
@@ -226,9 +226,9 @@
         send_own(z, low, length, held, cuts[0], 0, sems)
 
     def onward(part, z):
-        if part > 0:
-            send_own(z, low, length, held, cuts[part], part, sems)
         forward(z, low, length, held, cuts[part], part, sems)
+        if part + 1 < len(cuts):
+            send_own(z, low, length, held, cuts[part + 1], part + 1, sems)
 
     def exchange(part):
         return pltpu.make_async_remote_copy(
@@ -241,10 +241,8 @@
         )
 
     by_place(length, high, start)
-    by_place(length, high, functools.partial(onward, 0))
     for part, cols in enumerate(cuts):
-        if part + 1 < len(cuts):
-            by_place(length, high, functools.partial(onward, part + 1))
+        by_place(length, high, functools.partial(onward, part))
         for t in range(length):
             block = t * FAST + 1 - low
             hop_copy(held, block, cols, 0, part, sems, across).wait_recv()
@@ -279,7 +277,7 @@
             )
         )
     tiles = width // 128
-    pieces = min(4, tiles)
+    pieces = min(3, tiles)
     edges = [-(-tiles * i // pieces) * 128 for i in range(pieces)] + [width]
     cuts = [slice(edges[i], edges[i + 1]) for i in range(pieces)]
     part, other = pl.pallas_call(

time: 227 us -> 221 us (0.974)
  Pallas kernels: 206 us -> 199 us
    pallas_call x1, Pallas kernels: 65.2 us -> 58.3 us  [weight_grad(): pl.pallas_call(functools.partial(weight_kernel, devices // FAST, cuts), o...]
where the time goes in v5:
time: 221 us; the launch traced here: 220 us
  Pallas kernels  199 us (90%)
  other arithmetic  7.55 us (3%)
  matrix products  5.36 us (2%)
  blocking collectives  4.92 us (2%)
  local copies, waits for them, and re-layouts  2.54 us (1%)
    pallas_call x2, Pallas kernels, scatter_label(): pl.pallas_call(functools.partial(scatter_kernel, length, swap), out_shape...  91.9 us
    pallas_call x1, Pallas kernels, weight_grad(): pl.pallas_call(functools.partial(weight_kernel, devices // FAST, cuts), o...  58.3 us
    pallas_call x1, Pallas kernels, gather_score(): pl.pallas_call(functools.partial(score_kernel, devices // FAST), out_shap...  49 us

profile of v5, /device:TPU:0, one launch (start us, length us, event | category | flops | bytes accessed | tf_op | source)
XLA Modules:
  0.0 220.3 jit_solution(2305802037575842155)
XLA Ops:
  0.6 0.0 copy-start
  0.7 0.8 broadcast_multiply_fusion.1
  1.5 0.7 add_bitcast_fusion
  2.2 3.3 %convolution_convert_fusion.1 = bf16[1024,1792]{1,0:T(8,128)(2,1)S(1)} fusion(bf16[1024,448]{0,1:T(8,128)(2,1)} %param.7, bf16[448,1792]{1,0:T(8,128)(2,1)S(1)} %copy-done), kind=kOutput, calls=%fused_computation.1 | convolution fusion | flops 1646002176 | bytes 6193152 | tf_op jit(solution)/shard_map/dot_general | solution.py:500
  5.5 0.0 copy-start.3
  5.5 46.4 %shard_map.86 = f32[128,1792]{1,0:T(8,128)S(1)} custom-call(bf16[8,128,1792]{2,1,0:T(8,128)(2,1)S(1)} %bitcast.25), custom_call_target="tpu_custom_call" | custom-call | tf_op jit(solution)/shard_map/pallas_call | solution.py:458
  51.9 0.1 multiply_reduce_fusion.1
  52.0 2.5 %psum.14 = f32[128]{0:T(128)S(1)} all-reduce(f32[128]{0:T(128)S(1)} %multiply_reduce_fusion.1), channel_id=1, replica_groups=mesh['dp'=2,'label'=8,'tensor'=2] {'tensor'}, use_global_device_ids=true, to_apply=%region_1.2 | all-reduce | flops 128 | bytes 1024 | tf_op jit(solution)/shard_map/psum | solution.py:502
  54.5 0.1 multiply_convert_fusion.1.rows_ref
  54.7 0.0 copy-start.1
  54.7 1.5 copy-done.1
  56.2 49.0 %shard_map.87 = (bf16[8,128,1792]{2,1,0:T(8,128)(2,1)S(1)}, s32[8,16,128]{2,1,0:T(8,128)S(1)}, f32[8,128,512]{2,1,0:T(8,128)S(1)}) custom-call(bf16[128,1792]{1,0:T(8,128)(2,1)S(1)} %multiply_convert_fusion.1.rows_ref, s32[16,128]{1,0:T(8,128)S(1)} %pad.4.target_ref, bf16[512,1792]{1,0:T(8,128)(2,1)S(1)} %bitcast.27), custom_call_target="tpu_custom_call" | custom-call | tf_op jit(solution)/shard_map/pallas_call | solution.py:193
  105.2 0.1 slice_reduce_fusion.1
  105.3 1.8 select_convert_fusion.1
  107.1 0.1 pad_maximum_fusion.refs_1_
  107.2 2.1 convolution_convert_fusion
  109.3 45.6 %shard_map.88 = (f32[128,1792]{1,0:T(8,128)S(1)}, f32[2,128,1792]{2,1,0:T(8,128)S(1)}, bf16[2,128,1792]{2,1,0:T(8,128)(2,1)S(1)}) custom-call(bf16[8,128,1792]{2,1,0:T(8,128)(2,1)S(1)} %bitcast.24, bf16[1024,512]{1,0:T(8,128)(2,1)S(1)} %pad_maximum_fusion.refs_1_, bf16[1024,1792]{1,0:T(8,128)(2,1)S(1)} %bitcast.23), custom_call_target="tpu_custom_call" | custom-call | tf_op jit(solution)/shard_map/pallas_call | solution.py:458
  154.8 1.4 convert_add_fusion.1
  156.2 0.2 multiply_reduce_fusion
  156.4 2.5 %psum.15 = f32[128]{0:T(128)S(1)} all-reduce(f32[128]{0:T(128)S(1)} %multiply_reduce_fusion), channel_id=1, replica_groups=mesh['dp'=2,'label'=8,'tensor'=2] {'tensor'}, use_global_device_ids=true, to_apply=%region_5.6 | all-reduce | flops 128 | bytes 1024 | tf_op jit(solution)/shard_map/psum | solution.py:537
  158.9 0.2 multiply_convert_fusion.grad_ref
  159.1 0.9 copy-done.2
  160.0 58.3 %shard_map.89 = (f32[448,1792]{1,0:T(8,128)S(1)}, bf16[448,1792]{1,0:T(8,128)(2,1)S(1)}) custom-call(bf16[128,1792]{1,0:T(8,128)(2,1)S(1)} %multiply_convert_fusion.grad_ref, bf16[448,1024]{1,0:T(8,128)(2,1)S(1)} %bitcast.29), custom_call_target="tpu_custom_call" | custom-call | tf_op jit(solution)/shard_map/pallas_call | solution.py:283
  218.3 2.0 convert_add_fusion
  (10 shorter events, 0.1 us)
Async XLA Ops:
  0.6 1.6 copy-start
  5.5 49.0 %copy-start.3 = (f32[1792]{0:T(1024)S(1)}, f32[1792]{0:T(1024)}, u32[]{:S(2)}) copy-start(f32[1792]{0:T(1024)} %param.9) | copy-start | bytes 21508
  54.7 1.5 copy-start.1
  158.9 1.2 copy-start.2
